TPU v7x, 128 devices: a whole 4x4x4 slice. The times are simulated.
128 devices in a mesh: table: 4 (over y_lo, core), dp: 32 (over z, x, y_hi).
Axes of the slice: x: 4, y: 4 (y_hi: 2, y_lo: 2; y = y_hi * 2 + y_lo), z: 4, core: 2. Of those that a mesh axis runs over, the one named last changes fastest.
Arguments:
- table: float32 [1048576, 256], P(('table', 'dp')), may hold values from -6 to 6
- feature_owner: int32 [16384, 8], P(('table', 'dp')), may hold values from 0 to 127, all different within a row; in each aligned block of 128 rows (0 to 127, 128 to 255, ...) at most 16 rows name the same one
- feature_offset: int32 [16384, 8], P(('table', 'dp')), may hold values from 0 to 8191
- query_in: bfloat16 [256, 1024], replicated, may hold values from -0.375 to 0.375
- query_out: bfloat16 [1024, 256], replicated, may hold values from -0.1875 to 0.1875
- item_in: bfloat16 [256, 1024], replicated, may hold values from -0.375 to 0.375
- item_out: bfloat16 [1024, 256], replicated, may hold values from -0.1875 to 0.1875
Outputs:
- loss: float32 [16384], P(('table', 'dp'))
- table_grad: float32 [1048576, 256], P(('table', 'dp'))
- query_in_grad: float32 [256, 1024], replicated
- query_out_grad: float32 [1024, 256], replicated
- item_in_grad: float32 [256, 1024], replicated
- item_out_grad: float32 [1024, 256], replicated
Inputs may be any that keep to these rules, and one draw needn't show every extreme that they name: `feature_owner`: the 8 ids of a pair lie on different devices. Among the rows of one device no device index appears more than 16 times, and 16 is reached.
All inputs are finite; a program needn't handle non-finite values.
Results may differ from a plain program's by a relative error of at most 0.022.
Values may be sent and summed in bfloat16 or wider, within the bound.
A program may use at most 128 MiB of HBM per device.

v0:
```python
import jax
import jax.numpy as jnp
from jax import lax
from jax.sharding import PartitionSpec as P

score_scale = 20.0


def tower(inputs, w_in, w_out):
    pre_act = jnp.dot(inputs, w_in, preferred_element_type=jnp.float32)
    hidden = jax.nn.silu(pre_act).astype(jnp.bfloat16)
    output = jnp.dot(hidden, w_out, preferred_element_type=jnp.float32)
    out_norm = jnp.sqrt(jnp.sum(output * output, axis=-1, keepdims=True) + 1e-06)
    return (pre_act, hidden, out_norm, output / out_norm)


def tower_back(inputs, w_in, w_out, saved, grad_unit):
    pre_act, hidden, out_norm, unit = saved
    grad_output = (
        (grad_unit - unit * jnp.sum(grad_unit * unit, axis=-1, keepdims=True)) / out_norm
    ).astype(jnp.bfloat16)
    grad_w_out = jnp.dot(hidden.T, grad_output, preferred_element_type=jnp.float32)
    grad_hidden = jnp.dot(grad_output, w_out.T, preferred_element_type=jnp.float32)
    sigmoid_a = jax.nn.sigmoid(pre_act)
    grad_pre = (grad_hidden * sigmoid_a * (1.0 + pre_act * (1.0 - sigmoid_a))).astype(jnp.bfloat16)
    grad_w_in = jnp.dot(inputs.T, grad_pre, preferred_element_type=jnp.float32)
    grad_inputs = jnp.dot(grad_pre, w_in.T, preferred_element_type=jnp.float32)
    return (grad_w_in, grad_w_out, grad_inputs)


def local(table, feature_owner, feature_offset, query_in, query_out, item_in, item_out):
    pair_count = feature_owner.shape[0]
    per_pair = feature_owner.shape[1]
    bag_size = per_pair // 2
    feat_width = table.shape[1]
    table_devs = lax.axis_size("table")
    group_devs = lax.axis_size("dp")
    shards = table_devs * group_devs
    id_count = pair_count * per_pair
    slot_cap = 2 * id_count // shards
    flat_owner = feature_owner.reshape(-1)
    flat_offset = feature_offset.reshape(-1)
    one_hot = (flat_owner[:, None] == jnp.arange(shards, dtype=jnp.int32)[None, :]).astype(
        jnp.int32
    )
    slot_rank = jnp.sum((jnp.cumsum(one_hot, axis=0) - 1) * one_hot, axis=1)
    position = flat_owner * slot_cap + slot_rank
    requests = (
        jnp.zeros((shards * slot_cap,), jnp.int32)
        .at[position]
        .set(flat_offset)
        .reshape(shards, slot_cap)
    )
    asked_piece = lax.all_to_all(requests, ("table", "dp"), split_axis=0, concat_axis=0, tiled=True)
    looked_up = table[asked_piece].astype(jnp.bfloat16)
    fetched = lax.all_to_all(looked_up, ("table", "dp"), split_axis=0, concat_axis=0, tiled=True)
    pair_rows = fetched.reshape(shards * slot_cap, feat_width)[position].reshape(
        pair_count, per_pair, feat_width
    )
    query_x = jnp.sum(pair_rows[:, :bag_size].astype(jnp.float32), axis=1).astype(jnp.bfloat16)
    item_x = jnp.sum(pair_rows[:, bag_size:].astype(jnp.float32), axis=1).astype(jnp.bfloat16)
    q_saved = tower(query_x, query_in, query_out)
    k_saved = tower(item_x, item_in, item_out)
    query_unit = q_saved[3].astype(jnp.bfloat16)
    item_unit = k_saved[3].astype(jnp.bfloat16)
    all_items = lax.all_gather(item_unit, "dp", axis=0, tiled=True)
    scores = score_scale * jnp.dot(query_unit, all_items.T, preferred_element_type=jnp.float32)
    log_total = jnp.log(jnp.sum(jnp.exp(scores), axis=1))
    own_start = lax.axis_index("dp") * pair_count
    own_part = lax.dynamic_slice_in_dim(scores, own_start, pair_count, 1)
    loss = log_total - jnp.diagonal(own_part)
    soft = jnp.exp(scores - log_total[:, None]).astype(jnp.bfloat16)
    grad_query = score_scale * (
        jnp.dot(soft, all_items, preferred_element_type=jnp.float32) - item_unit.astype(jnp.float32)
    )
    summed = lax.psum_scatter(
        jnp.dot(soft.T, query_unit, preferred_element_type=jnp.float32).astype(jnp.bfloat16),
        "dp",
        scatter_dimension=0,
        tiled=True,
    ).astype(jnp.float32)
    grad_item = score_scale * (summed - query_unit.astype(jnp.float32))
    q_win, q_wout, q_dx = tower_back(query_x, query_in, query_out, q_saved, grad_query)
    k_win, k_wout, k_dx = tower_back(item_x, item_in, item_out, k_saved, grad_item)
    q_win, q_wout, k_win, k_wout = lax.psum((q_win, q_wout, k_win, k_wout), ("table", "dp"))
    row_grads = jnp.concatenate(
        [
            jnp.broadcast_to(q_dx[:, None, :], (pair_count, bag_size, feat_width)),
            jnp.broadcast_to(k_dx[:, None, :], (pair_count, bag_size, feat_width)),
        ],
        axis=1,
    )
    grad_slots = (
        jnp.zeros((shards * slot_cap, feat_width), jnp.float32)
        .at[position]
        .set(row_grads.reshape(-1, feat_width))
    )
    returned = lax.all_to_all(
        grad_slots.reshape(shards, slot_cap, feat_width).astype(jnp.bfloat16),
        ("table", "dp"),
        split_axis=0,
        concat_axis=0,
        tiled=True,
    ).astype(jnp.float32)
    table_grad = (
        jnp.zeros(table.shape, jnp.float32)
        .at[asked_piece.reshape(-1)]
        .add(returned.reshape(-1, feat_width))
    )
    return (loss, table_grad, q_win, q_wout, k_win, k_wout)


def solution(mesh):
    in_specs = (
        P(("table", "dp"), None),
        P(("table", "dp"), None),
        P(("table", "dp"), None),
        P(),
        P(),
        P(),
        P(),
    )
    out_specs = (P(("table", "dp")), P(("table", "dp"), None), P(), P(), P(), P())
    return jax.shard_map(local, mesh=mesh, in_specs=in_specs, out_specs=out_specs, check_vma=False)
```

profile of v0, /device:TPU:1, one launch (start us, length us, event | category | flops | bytes accessed | tf_op | source)
XLA Modules:
  0.0 515.4 jit_solution(13545192990639093152)
XLA Ops:
  7.2 0.7 broadcast_multiply_fusion
  7.9 0.8 copy.20
  9.2 0.8 copy.24
  10.5 0.4 fusion.12
  10.9 4.3 scatter_custom_fusion
  15.3 21.1 %all_to_all.22 = s32[128,1,16]{2,1,0:T(1,128)S(1)} all-to-all(s32[128,1,16]{2,1,0:T(1,128)S(1)} %bitcast.57), channel_id=1, replica_groups=mesh['table'=4,'dp'=32] {'table','dp'}, dimensions={0} | all-to-all | bytes 16384 | tf_op jit(solution)/shard_map/all_to_all | solution.py:54
  36.4 0.6 copy-done.5
  37.1 11.9 %gather_fusion = bf16[2048,256]{1,0:T(8,128)(2,1)} fusion(f32[8192,256]{1,0:T(8,128)} %param.7, s32[2048]{0:T(1024)S(1)} %broadcast_clamp_fusion), kind=kCustom, calls=%fused_computation | custom fusion | bytes 2105344 | tf_op jit(solution)/shard_map/gather | solution.py:55
  49.0 4.3 all-to-all-start.1
  53.4 19.3 %all-to-all-done.1 = bf16[128,16,256]{2,1,0:T(8,128)(2,1)S(1)} async-done(((bf16[128,16,256]{2,1,0:T(8,128)(2,1)}), bf16[128,16,256]{2,1,0:T(8,128)(2,1)S(1)}, u32[]{:S(2)}, u32[]{:S(2)}) %all-to-all-start.1) | async-done | bytes 1048608 | tf_op jit(solution)/shard_map/all_to_all | solution.py:56
  72.7 3.9 gather_fusion.1
  76.7 0.6 slice_reduce_fusion
  77.3 1.0 multiply_convert_fusion
  78.3 0.3 multiply_reduce_fusion.2
  78.7 0.7 fusion.19
  79.5 1.0 multiply_convert_fusion.1
  80.5 0.3 multiply_reduce_fusion.3
  81.0 64.1 %all-gather.2.cloned.1.call-done = bf16[4096,256]{1,0:T(8,128)(2,1)} async-done(((bf16[128,256]{1,0:T(8,128)(2,1)}), bf16[4096,256]{1,0:T(8,128)(2,1)}) %all-gather.2.cloned.1.call-update) | async-done | bytes 2097168 | tf_op jit(solution)/shard_map/all_gather | solution.py:66
  145.1 3.0 exponential_reduce_fusion
  148.2 1.8 gather_fusion.2
  149.9 1.2 fusion.22
  151.1 2.1 convolution_convert_fusion
  153.5 0.6 copy-done.4
  154.1 2.3 multiply_reduce_fusion.1
  156.4 0.4 fusion.5
  156.8 0.4 copy-done.16
  157.2 1.3 fusion.25
  158.5 1.3 fusion.20
  159.9 155.6 %reduce-scatter.2.cloned.1.call-done = bf16[128,256]{1,0:T(8,128)(2,1)} async-done(((bf16[4096,256]{1,0:T(8,128)(2,1)}), bf16[128,256]{1,0:T(8,128)(2,1)}) %reduce-scatter.2.cloned.1.call-update) | async-done | bytes 65552 | tf_op jit(solution)/shard_map/reduce_scatter | solution.py:76
  315.4 1.0 multiply_reduce_fusion
  316.5 1.3 fusion.6
  317.8 1.3 fusion.26
  319.1 1.4 fusion.21
  320.5 0.3 fusion.23
  320.8 0.7 copy-done.8
  321.9 0.9 broadcast_in_dim.15
  322.8 5.9 %scatter_custom_fusion.1 = f32[2048,256]{1,0:T(8,128)S(1)} fusion(s32[1024]{0:T(1024)S(1)} %bitcast.61, f32[128,4,256]{2,1,0:T(4,128)} %broadcast_in_dim.15, f32[]{:T(128)} %constant.64, f32[128,4,256]{2,1,0:T(4,128)S(1)} %broadcast_in_dim.14, f32[]{:T(128)} %constant.20.clone.1), kind=kCustom, calls=%fused_computation.22 | custom fusion | flops 262144 | bytes 3145736 | tf_op jit(solution)/shard_map/scatter | solution.py:96
  328.7 1.1 convert_element_type.73
  329.7 27.7 %all-to-all-start.2 = ((bf16[128,16,256]{2,1,0:T(8,128)(2,1)}), bf16[128,16,256]{2,1,0:T(8,128)(2,1)S(1)}, u32[]{:S(2)}, u32[]{:S(2)}) async-start(bf16[128,16,256]{2,1,0:T(8,128)(2,1)} %bitcast.54), calls=%async_computation.3 | async-start | bytes 2097152 | tf_op jit(solution)/shard_map/all_to_all | solution.py:98
  357.4 0.5 broadcast.164
  358.0 0.8 reduce.5
  358.9 20.0 %all-to-all-done.2 = bf16[128,16,256]{2,1,0:T(8,128)(2,1)S(1)} async-done(((bf16[128,16,256]{2,1,0:T(8,128)(2,1)}), bf16[128,16,256]{2,1,0:T(8,128)(2,1)S(1)}, u32[]{:S(2)}, u32[]{:S(2)}) %all-to-all-start.2) | async-done | bytes 1048608 | tf_op jit(solution)/shard_map/all_to_all | solution.py:98
  378.9 16.1 %scatter_custom_fusion.2 = f32[8192,256]{1,0:T(8,128)} fusion(s32[2048]{0:T(1024)S(1)} %bitcast.62, f32[]{:T(128)} %constant.20.clone.1, bf16[2048,256]{1,0:T(8,128)(2,1)S(1)} %bitcast.53), kind=kCustom, calls=%fused_computation.8 | custom fusion | flops 1048576 | bytes 9437188 | tf_op jit(solution)/shard_map/scatter-add | solution.py:108
  395.0 108.5 %all-reduce.3.cloned.1.call-done = (f32[256,1024]{1,0:T(8,128)}, f32[1024,256]{1,0:T(8,128)}, f32[256,1024]{1,0:T(8,128)}, f32[1024,256]{1,0:T(8,128)}) async-done(((f32[256,1024]{1,0:T(8,128)}, f32[1024,256]{1,0:T(8,128)}, f32[256,1024]{1,0:T(8,128)}, f32[1024,256]{1,0:T(8,128)}), (f32[256,1024]{1,0:T(8,128)}, f32[1024,256]{1,0:T(8,128)}, f32[256,1024]{1,0:T(8,128)}, ...) | async-done | bytes 4194320 | tf_op jit(solution)/shard_map/psum | solution.py:85
  503.5 2.5 copy.30
  505.9 1.0 copy.31
  506.9 1.0 copy.32
  507.9 1.0 copy.33
  (69 shorter events, 2.2 us)
Async XLA Ops:
  7.2 72.3 %copy-start = (bf16[256,1024]{1,0:T(8,128)(2,1)S(1)}, bf16[256,1024]{1,0:T(8,128)(2,1)}, u32[]{:S(2)}) copy-start(bf16[256,1024]{1,0:T(8,128)(2,1)} %param.10) | copy-start | bytes 1572868
  36.4 0.6 copy-start.5
  49.0 23.7 %all-to-all-start.1 = ((bf16[128,16,256]{2,1,0:T(8,128)(2,1)}), bf16[128,16,256]{2,1,0:T(8,128)(2,1)S(1)}, u32[]{:S(2)}, u32[]{:S(2)}) async-start(bf16[128,16,256]{2,1,0:T(8,128)(2,1)} %bitcast.7), calls=%async_computation.1 | async-start | bytes 2097152 | tf_op jit(solution)/shard_map/all_to_all | solution.py:56
  53.3 91.8 %all-gather.2.cloned.1.call-start = ((), (), s32[]{:S(2)}) async-start(), calls=%async_computation.4 | async-start | bytes 2162688 | tf_op jit(solution)/shard_map/all_gather | solution.py:66
  72.7 4.6 copy-start.7
  76.7 1.7 copy-start.11
  77.3 3.3 copy-start.13
  77.3 3.3 copy-start.15
  78.3 2.2 copy-start.9
  79.4 236.0 %reduce-scatter.2.cloned.1.call-start = ((), (), s32[]{:S(2)}) async-start(), calls=%async_computation.5 | async-start | bytes 2162688 | tf_op jit(solution)/shard_map/reduce_scatter | solution.py:76
  153.3 0.8 copy-start.4
  153.3 350.2 %all-reduce.3.cloned.1.call-start = ((), (), s32[]{:S(2)}) async-start(), calls=%async_computation.6 | async-start | bytes 8388608 | tf_op jit(solution)/shard_map/psum | solution.py:85
  154.1 2.3 copy-start.10
  154.1 2.3 copy-start.19
  156.4 0.8 copy-start.16
  157.2 159.2 %copy-start.12 = (bf16[1024,256]{1,0:T(8,128)(2,1)S(1)}, bf16[1024,256]{1,0:T(8,128)(2,1)}, u32[]{:S(2)}) copy-start(bf16[1024,256]{1,0:T(8,128)(2,1)} %param.13) | copy-start | bytes 1572868
  157.2 159.2 %copy-start.18 = (f32[128,1024]{1,0:T(8,128)S(1)}, f32[128,1024]{1,0:T(8,128)}, u32[]{:S(2)}) copy-start(f32[128,1024]{1,0:T(8,128)} %get-tuple-element.19) | copy-start | bytes 1572868
  316.5 1.3 copy-start.14
  316.5 2.6 copy-start.17
  320.4 1.0 copy-start.8
  328.6 29.3 %copy-start.6 = (s32[128,1,16]{2,1,0:T(1,128)S(1)}, s32[128,1,16]{2,1,0:T(1,128)}, u32[]{:S(2)}) copy-start(s32[128,1,16]{2,1,0:T(1,128)} %copy-done.5) | copy-start | bytes 24580
  329.7 49.1 %all-to-all-start.2 = ((bf16[128,16,256]{2,1,0:T(8,128)(2,1)}), bf16[128,16,256]{2,1,0:T(8,128)(2,1)S(1)}, u32[]{:S(2)}, u32[]{:S(2)}) async-start(bf16[128,16,256]{2,1,0:T(8,128)(2,1)} %bitcast.54), calls=%async_computation.3 | async-start | bytes 2097152 | tf_op jit(solution)/shard_map/all_to_all | solution.py:98
  503.5 2.5 copy-start.3
  503.5 3.4 copy-start.2
  505.9 1.9 copy-start.1
Sparse Core Ops, SparseCore 0:
  79.5 65.5 all-gather.1
  153.4 161.9 reduce-scatter.1
  322.5 180.9 all-reduce.2
where the time goes:
time: 516 us; the launch traced here: 515 us
  waiting for transfers between devices  368 us (71%)
  local copies, waits for them, and re-layouts  33.7 us (7%)
  starting transfers between devices  32.3 us (6%)
  other arithmetic  28.9 us (6%)
  blocking collectives  21.1 us (4%)
  matrix products  17.7 us (3%)
  between operations  14.1 us (3%)
    reduce_scatter x1, waiting for transfers between devices, local(): lax.psum_scatter(jnp.dot(soft.T, query_unit, preferred_element_type=jnp.f...  156 us
    psum x1, waiting for transfers between devices, local(): lax.psum((q_win, q_wout, k_win, k_wout), ('table', 'dp'))  109 us
    all_gather x1, waiting for transfers between devices, local(): all_items = lax.all_gather(item_unit, 'dp', axis=0, tiled=True)  64.1 us
    all_to_all x1, starting transfers between devices, local(): lax.all_to_all(grad_slots.reshape(shards, slot_cap, feat_width).astype(jn...  27.7 us
    all_to_all x1, blocking collectives, local(): lax.all_to_all(requests, ('table', 'dp'), split_axis=0, concat_axis=0, ti...  21.1 us
    all_to_all x1, waiting for transfers between devices, local(): lax.all_to_all(grad_slots.reshape(shards, slot_cap, feat_width).astype(jn...  20 us
    all_to_all x1, waiting for transfers between devices, local(): lax.all_to_all(looked_up, ('table', 'dp'), split_axis=0, concat_axis=0, t...  19.3 us
    scatter-add x1, other arithmetic, local(): table_grad = jnp.zeros(table.shape, jnp.float32).at[asked_piece.reshape(-...  16.1 us
  transfers between devices with their start and end apart: 5, of which 5 were waited for; matrix products, arithmetic and copies ran while one was open for 6% of the time, Pallas kernels for 0%

commit v1 on v0

--- a/solution.py
+++ b/solution.py
@@ -1,9 +1,101 @@
+import functools
+
 import jax
 import jax.numpy as jnp
 from jax import lax
+from jax.experimental import pallas as pl
+from jax.experimental.pallas import tpu as pltpu
 from jax.sharding import PartitionSpec as P
 
 score_scale = 20.0
+MESH = pl.DeviceIdType.MESH
+CAP = 16
+
+
+def fetch_kernel(
+    shards, group, requests, table_ref, fetched, asked,
+    table_rows, rows, stage, asked_scalars, table_sem, id_sems, scalar_sem, row_sems,
+):
+    me = lax.axis_index("table") * group + lax.axis_index("dp")
+    load = pltpu.make_async_copy(table_ref, table_rows, table_sem)
+    load.start()
+
+    def place(device):
+        return (lax.div(device, group), lax.rem(device, group))
+
+    barrier = pltpu.get_barrier_semaphore()
+
+    @pl.loop(1, shards)
+    def _(step):
+        pl.semaphore_signal(
+            barrier, inc=1, device_id=place(lax.rem(me + step, shards)), device_id_type=MESH
+        )
+
+    pl.semaphore_wait(barrier, shards - 1)
+    pltpu.make_async_copy(requests.at[me], asked.at[me], scalar_sem).start()
+
+    @pl.loop(1, shards)
+    def _(step):
+        owner = lax.rem(me + step, shards)
+        pltpu.make_async_remote_copy(
+            requests.at[owner], asked.at[me], id_sems.at[0], id_sems.at[1],
+            device_id=place(owner), device_id_type=MESH,
+        ).start()
+
+    others = pl.ds(0, shards - 1)
+    pltpu.make_async_copy(requests.at[me], asked.at[me], scalar_sem).wait()
+    pltpu.make_async_copy(asked.at[others], asked.at[others], id_sems.at[1]).wait()
+    spread = pltpu.make_async_copy(asked, asked_scalars, scalar_sem)
+    spread.start()
+    load.wait()
+    spread.wait()
+
+    def lookup(asker):
+        for slot in range(CAP):
+            stage[slot : slot + 1, :] = table_rows[pl.ds(asked_scalars[asker, 0, slot], 1), :]
+        return stage[...].astype(jnp.bfloat16)
+
+    @pl.loop(1, shards)
+    def _(step):
+        asker = lax.rem(me + step, shards)
+        rows[asker] = lookup(asker)
+        pltpu.make_async_remote_copy(
+            rows.at[asker], fetched.at[me], row_sems.at[0], row_sems.at[1],
+            device_id=place(asker), device_id_type=MESH,
+        ).start()
+
+    fetched[me] = lookup(me)
+    pltpu.make_async_copy(requests.at[others], requests.at[others], id_sems.at[0]).wait()
+    pltpu.make_async_copy(rows.at[others], rows.at[others], row_sems.at[1]).wait()
+    pltpu.make_async_copy(rows.at[others], rows.at[others], row_sems.at[0]).wait()
+
+
+def fetch(requests, table):
+    group = lax.axis_size("dp")
+    shards = lax.axis_size("table") * group
+    width = table.shape[1]
+    return pl.pallas_call(
+        functools.partial(fetch_kernel, shards, group),
+        out_shape=(
+            jax.ShapeDtypeStruct((shards, CAP, width), jnp.bfloat16),
+            jax.ShapeDtypeStruct((shards, 1, 128), jnp.int32),
+        ),
+        in_specs=[pl.BlockSpec(memory_space=pltpu.VMEM), pl.BlockSpec(memory_space=pl.ANY)],
+        out_specs=(pl.BlockSpec(memory_space=pltpu.VMEM),) * 2,
+        scratch_shapes=[
+            pltpu.VMEM(table.shape, jnp.float32),
+            pltpu.VMEM((shards, CAP, width), jnp.bfloat16),
+            pltpu.VMEM((CAP, width), jnp.float32),
+            pltpu.SMEM((shards, 1, 128), jnp.int32),
+            pltpu.SemaphoreType.DMA,
+            pltpu.SemaphoreType.DMA((2,)),
+            pltpu.SemaphoreType.DMA,
+            pltpu.SemaphoreType.DMA((2,)),
+        ],
+        compiler_params=pltpu.CompilerParams(
+            collective_id=0, has_side_effects=True, vmem_limit_bytes=24 << 20
+        ),
+    )(requests, table)
 
 
 def tower(inputs, w_in, w_out):
@@ -51,9 +143,10 @@
         .set(flat_offset)
         .reshape(shards, slot_cap)
     )
-    asked_piece = lax.all_to_all(requests, ("table", "dp"), split_axis=0, concat_axis=0, tiled=True)
-    looked_up = table[asked_piece].astype(jnp.bfloat16)
-    fetched = lax.all_to_all(looked_up, ("table", "dp"), split_axis=0, concat_axis=0, tiled=True)
+    fetched, asked = fetch(
+        jnp.pad(requests, ((0, 0), (0, 128 - slot_cap))).reshape(shards, 1, 128), table
+    )
+    asked_piece = asked[:, 0, :slot_cap]
     pair_rows = fetched.reshape(shards * slot_cap, feat_width)[position].reshape(
         pair_count, per_pair, feat_width
     )

time: 516 us -> 497 us (0.963)
  Pallas kernels: 0 us -> 34.3 us
  blocking collectives: 21.1 us -> 0 us
  waiting for transfers between devices: 368 us -> 352 us
  local copies, waits for them, and re-layouts: 33.7 us -> 23.6 us
    pallas_call x0 -> x1, Pallas kernels: none -> 34.3 us  [fetch(): pl.pallas_call(functools.partial(fetch_kernel, shards, group), out_shape=...]
    all_to_all x1 -> x0, blocking collectives: 21.1 us -> none  [local(): lax.all_to_all(requests, ('table', 'dp'), split_axis=0, concat_axis=0, ti...]
    all_to_all x1 -> x0, waiting for transfers between devices: 19.3 us -> none  [local(): lax.all_to_all(looked_up, ('table', 'dp'), split_axis=0, concat_axis=0, t...]
    gather x1 -> x0, local copies, waits for them, and re-layouts: 11.9 us -> none  [local(): looked_up = table[asked_piece].astype(jnp.bfloat16)]
    unnamed x46 -> x40, local copies, waits for them, and re-layouts: 9.36 us -> 12.1 us
  transfers between devices with their start and end apart: 5 -> 4, of which waited for: 5 -> 4; matrix products, arithmetic and copies ran while one was open for 6% -> 6% of each run, Pallas kernels for 0% -> 0%
where the time goes in v1:
time: 497 us; the launch traced here: 496 us
  waiting for transfers between devices  352 us (71%)
  Pallas kernels  34.3 us (7%)
  starting transfers between devices  28.2 us (6%)
  other arithmetic  26.9 us (5%)
  local copies, waits for them, and re-layouts  23.6 us (5%)
  matrix products  17.1 us (3%)
  between operations  14.1 us (3%)
    reduce_scatter x1, waiting for transfers between devices, local(): lax.psum_scatter(jnp.dot(soft.T, query_unit, preferred_element_type=jnp.f...  156 us
    psum x1, waiting for transfers between devices, local(): lax.psum((q_win, q_wout, k_win, k_wout), ('table', 'dp'))  109 us
    all_gather x1, waiting for transfers between devices, local(): all_items = lax.all_gather(item_unit, 'dp', axis=0, tiled=True)  66.3 us
    pallas_call x1, Pallas kernels, fetch(): pl.pallas_call(functools.partial(fetch_kernel, shards, group), out_shape=...  34.3 us
    all_to_all x1, starting transfers between devices, local(): lax.all_to_all(grad_slots.reshape(shards, slot_cap, feat_width).astype(jn...  28.1 us
    all_to_all x1, waiting for transfers between devices, local(): lax.all_to_all(grad_slots.reshape(shards, slot_cap, feat_width).astype(jn...  21.1 us
    scatter-add x1, other arithmetic, local(): table_grad = jnp.zeros(table.shape, jnp.float32).at[asked_piece.reshape(-...  15.6 us
    unnamed x40, local copies, waits for them, and re-layouts  12.1 us
  transfers between devices with their start and end apart: 4, of which 4 were waited for; matrix products, arithmetic and copies ran while one was open for 6% of the time, Pallas kernels for 0%

profile of v1, /device:TPU:1, one launch (start us, length us, event | category | flops | bytes accessed | tf_op | source)
XLA Modules:
  0.0 496.4 jit_solution(14369813570043103564)
XLA Ops:
  7.2 0.7 broadcast_multiply_fusion
  8.0 0.8 copy.14
  9.2 0.8 copy.18
  10.1 0.2 fusion.13
  10.4 0.1 copy.17
  10.5 0.4 fusion.12
  10.9 4.3 scatter_custom_fusion
  15.4 3.4 copy-done.1
  18.7 34.3 %shard_map.118 = (bf16[128,16,256]{2,1,0:T(8,128)(2,1)S(1)}, s32[128,1,128]{2,1,0:T(1,128)S(1)}) custom-call(s32[128,1,128]{2,1,0:T(1,128)S(1)} %bitcast.49, f32[8192,256]{1,0:T(8,128)S(1)} %copy-done.1), custom_call_target="tpu_custom_call" | custom-call | tf_op jit(solution)/shard_map/pallas_call | solution.py:77
  53.0 3.9 gather_fusion
  57.0 0.6 slice_reduce_fusion
  57.6 1.0 multiply_convert_fusion
  58.6 0.3 multiply_reduce_fusion.2
  59.0 0.7 fusion.19
  59.8 1.0 multiply_convert_fusion.1
  60.8 0.3 multiply_reduce_fusion.3
  61.2 0.1 fusion.18
  61.3 0.3 copy-done.5
  61.5 66.3 %all-gather.2.cloned.1.call-done = bf16[4096,256]{1,0:T(8,128)(2,1)} async-done(((bf16[128,256]{1,0:T(8,128)(2,1)}), bf16[4096,256]{1,0:T(8,128)(2,1)}) %all-gather.2.cloned.1.call-update) | async-done | bytes 2097168 | tf_op jit(solution)/shard_map/all_gather | solution.py:159
  127.8 2.5 exponential_reduce_fusion
  130.4 1.2 gather_fusion.1
  131.6 0.5 fusion.22
  132.1 2.1 convolution_convert_fusion
  134.3 0.8 copy-done.7
  135.1 2.3 multiply_reduce_fusion.1
  137.4 0.4 fusion.5
  137.8 1.3 fusion.25
  139.1 1.3 fusion.20
  140.5 155.8 %reduce-scatter.2.cloned.1.call-done = bf16[128,256]{1,0:T(8,128)(2,1)} async-done(((bf16[4096,256]{1,0:T(8,128)(2,1)}), bf16[128,256]{1,0:T(8,128)(2,1)}) %reduce-scatter.2.cloned.1.call-update) | async-done | bytes 65552 | tf_op jit(solution)/shard_map/reduce_scatter | solution.py:169
  296.2 1.0 multiply_reduce_fusion
  297.3 1.3 fusion.6
  298.6 1.3 fusion.26
  299.8 1.4 fusion.21
  301.2 0.3 fusion.23
  301.5 0.7 copy-done.9
  302.2 0.3 fusion.24
  302.7 0.9 broadcast_in_dim.15
  303.5 5.9 %scatter_custom_fusion.1 = f32[2048,256]{1,0:T(8,128)S(1)} fusion(s32[1024]{0:T(1024)S(1)} %bitcast.56, f32[128,4,256]{2,1,0:T(4,128)} %broadcast_in_dim.15, f32[]{:T(128)} %constant.64, f32[128,4,256]{2,1,0:T(4,128)S(1)} %broadcast_in_dim.14, f32[]{:T(128)} %constant.12.clone.1), kind=kCustom, calls=%fused_computation.21 | custom fusion | flops 262144 | bytes 3145736 | tf_op jit(solution)/shard_map/scatter | solution.py:189
  309.4 1.1 convert_element_type.69
  310.5 28.1 %all-to-all-start = ((bf16[128,16,256]{2,1,0:T(8,128)(2,1)}), bf16[128,16,256]{2,1,0:T(8,128)(2,1)S(1)}, u32[]{:S(2)}, u32[]{:S(2)}) async-start(bf16[128,16,256]{2,1,0:T(8,128)(2,1)} %bitcast.51), calls=%async_computation.1 | async-start | bytes 2097152 | tf_op jit(solution)/shard_map/all_to_all | solution.py:191
  338.6 0.2 slice_reduce_fusion.2
  338.8 21.1 %all-to-all-done = bf16[128,16,256]{2,1,0:T(8,128)(2,1)S(1)} async-done(((bf16[128,16,256]{2,1,0:T(8,128)(2,1)}), bf16[128,16,256]{2,1,0:T(8,128)(2,1)S(1)}, u32[]{:S(2)}, u32[]{:S(2)}) %all-to-all-start) | async-done | bytes 1048608 | tf_op jit(solution)/shard_map/all_to_all | solution.py:191
  360.0 15.6 %scatter_custom_fusion.2 = f32[8192,256]{1,0:T(8,128)} fusion(s32[2048]{0:T(1024)S(1)} %bitcast.57, f32[]{:T(128)} %constant.12.clone.1, bf16[2048,256]{1,0:T(8,128)(2,1)S(1)} %bitcast.50), kind=kCustom, calls=%fused_computation.7 | custom fusion | flops 1048576 | bytes 9437188 | tf_op jit(solution)/shard_map/scatter-add | solution.py:201
  375.5 109.0 %all-reduce.4.cloned.1.call-done = (f32[256,1024]{1,0:T(8,128)}, f32[1024,256]{1,0:T(8,128)}, f32[256,1024]{1,0:T(8,128)}, f32[1024,256]{1,0:T(8,128)}) async-done(((f32[256,1024]{1,0:T(8,128)}, f32[1024,256]{1,0:T(8,128)}, f32[256,1024]{1,0:T(8,128)}, f32[1024,256]{1,0:T(8,128)}), (f32[256,1024]{1,0:T(8,128)}, f32[1024,256]{1,0:T(8,128)}, f32[256,1024]{1,0:T(8,128)}, ...) | async-done | bytes 4194320 | tf_op jit(solution)/shard_map/psum | solution.py:178
  484.5 2.5 copy.23
  487.0 1.0 copy.24
  488.0 1.0 copy.25
  488.9 1.0 copy.26
  (57 shorter events, 1.2 us)
Async XLA Ops:
  7.2 52.6 %copy-start = (bf16[256,1024]{1,0:T(8,128)(2,1)S(1)}, bf16[256,1024]{1,0:T(8,128)(2,1)}, u32[]{:S(2)}) copy-start(bf16[256,1024]{1,0:T(8,128)(2,1)} %param.10) | copy-start | bytes 1572868
  7.2 120.6 %all-gather.2.cloned.1.call-start = ((), (), s32[]{:S(2)}) async-start(), calls=%async_computation.2 | async-start | bytes 2162688 | tf_op jit(solution)/shard_map/all_gather | solution.py:159
  15.3 3.4 copy-start.1
  53.0 4.6 copy-start.8
  57.0 1.6 copy-start.12
  58.6 2.2 copy-start.10
  59.7 236.5 %reduce-scatter.2.cloned.1.call-start = ((), (), s32[]{:S(2)}) async-start(), calls=%async_computation.3 | async-start | bytes 2162688 | tf_op jit(solution)/shard_map/reduce_scatter | solution.py:169
  60.8 0.7 copy-start.5
  134.3 0.8 copy-start.7
  134.3 350.2 %all-reduce.4.cloned.1.call-start = ((), (), s32[]{:S(2)}) async-start(), calls=%async_computation.4 | async-start | bytes 8388608 | tf_op jit(solution)/shard_map/psum | solution.py:178
  135.1 2.3 copy-start.11
  135.1 2.3 copy-start.16
  137.4 1.7 copy-start.6
  137.8 159.5 %copy-start.13 = (bf16[1024,256]{1,0:T(8,128)(2,1)S(1)}, bf16[1024,256]{1,0:T(8,128)(2,1)}, u32[]{:S(2)}) copy-start(bf16[1024,256]{1,0:T(8,128)(2,1)} %param.13) | copy-start | bytes 1572868
  137.8 159.5 %copy-start.15 = (f32[128,1024]{1,0:T(8,128)S(1)}, f32[128,1024]{1,0:T(8,128)}, u32[]{:S(2)}) copy-start(f32[128,1024]{1,0:T(8,128)} %get-tuple-element.23) | copy-start | bytes 1572868
  297.3 2.6 copy-start.14
  301.2 1.0 copy-start.9
  310.5 49.5 %all-to-all-start = ((bf16[128,16,256]{2,1,0:T(8,128)(2,1)}), bf16[128,16,256]{2,1,0:T(8,128)(2,1)S(1)}, u32[]{:S(2)}, u32[]{:S(2)}) async-start(bf16[128,16,256]{2,1,0:T(8,128)(2,1)} %bitcast.51), calls=%async_computation.1 | async-start | bytes 2097152 | tf_op jit(solution)/shard_map/all_to_all | solution.py:191
  484.5 2.5 copy-start.4
  484.5 3.4 copy-start.3
  487.0 1.9 copy-start.2
Sparse Core Ops, SparseCore 0:
  59.8 67.9 all-gather.1
  134.4 161.7 reduce-scatter.1
  303.3 181.2 all-reduce.3

commit v2 on v0

v2 whole, which is shorter than its diff:
```python
import jax
import jax.numpy as jnp
from jax import lax
from jax.experimental import pallas as pl
from jax.experimental.pallas import tpu as pltpu
from jax.sharding import PartitionSpec as P

MESH = pl.DeviceIdType.MESH
SCALE = 20.0
SHARDS = 128
GROUP = 32
CAP = 16
PAIRS = 128
WIDTH = 256
HIDDEN = 1024
ROWS = 8192
QUERY_PEERS = 8
ITEM_PEERS = 4
BLOCK_Q = QUERY_PEERS * PAIRS
BLOCK_K = ITEM_PEERS * PAIRS
GRAD_ROWS = 4 * HIDDEN
HALF = GRAD_ROWS // 2
PARTS = ((0, 768, (0, 1, 2)), (768, 768, (2, 0, 1)), (1536, 512, (1, 2, 0)))
f32 = jnp.float32
bf16 = jnp.bfloat16


def mm(a, b, contract=((1,), (0,))):
    return lax.dot_general(a, b, (contract, ((), ())), preferred_element_type=f32)


def step_kernel(
    owner_ref, offset_ref, table_ref, w_ins_ref, w_outs_ref, w_ini_ref, w_outi_ref,
    loss_ref, asked, returned, summed,
    table_rows, w_in, w_out, requests, asked_scalars, stage, rows, fetched, pick, pick_t,
    pre_act, hidden, unit, norm, queries, items, expo, soft, part_sums,
    q_send, q_recv, k_send, k_recv, slots, grads, core_recv, half, sum1, recv1, recv2, recv3,
    load_sems, send_sems, recv_sems, ring_send, ring_recv,
):
    t = lax.axis_index("table")
    dp = lax.axis_index("dp")
    me = t * GROUP + dp
    core = lax.rem(t, 2)
    z = lax.div(dp, QUERY_PEERS)
    a = lax.rem(dp, QUERY_PEERS)
    x = lax.div(a, 2)
    y = lax.rem(a, 2) * 2 + lax.div(t, 2)
    coords = (x, y, z)

    def place(device):
        return (lax.div(device, GROUP), lax.rem(device, GROUP))

    def chip(coords, core):
        cx, cy, cz = coords
        return (lax.rem(cy, 2) * 2 + core, cz * QUERY_PEERS + cx * 2 + lax.div(cy, 2))

    def send(src, dst, s_sem, r_sem, device):
        pltpu.make_async_remote_copy(
            src, dst, s_sem, r_sem, device_id=device, device_id_type=MESH
        ).start()

    def wait(ref, sem):
        pltpu.make_async_copy(ref, ref, sem).wait()

    loads = [
        pltpu.make_async_copy(src, dst, load_sems.at[i])
        for i, (src, dst) in enumerate(
            [
                (table_ref, table_rows),
                (w_ins_ref, w_in.at[0]),
                (w_outs_ref, w_out.at[0]),
                (w_ini_ref, w_in.at[1]),
                (w_outi_ref, w_out.at[1]),
            ]
        )
    ]
    for load in loads:
        load.start()

    barrier = pltpu.get_barrier_semaphore()

    @pl.loop(1, SHARDS)
    def _(step):
        pl.semaphore_signal(
            barrier, inc=1, device_id=place(lax.rem(me + step, SHARDS)), device_id_type=MESH
        )

    lane = lax.broadcasted_iota(jnp.int32, (PAIRS, SHARDS), 1)
    row = lax.broadcasted_iota(jnp.int32, (PAIRS, SHARDS), 0)
    names = [(owner_ref[:, k : k + 1] == lane).astype(jnp.int32) for k in range(8)]
    offsets = sum(names[k] * offset_ref[:, k : k + 1] for k in range(8))
    named_q = sum(names[:4])
    named_k = sum(names[4:])
    named = named_q + named_k
    rank = named
    for shift in (1, 2, 4, 8, 16, 32, 64):
        rank = rank + jnp.where(row >= shift, pltpu.roll(rank, shift, 0), 0)
    rank = rank - named
    by_slot = [
        jnp.sum(jnp.where(rank == r, offsets, 0), axis=0, keepdims=True) for r in range(CAP)
    ] + [jnp.sum(named, axis=0, keepdims=True)]
    by_slot = jnp.concatenate(
        by_slot + [jnp.zeros((SHARDS - CAP - 1, SHARDS), jnp.int32)], axis=0
    )
    requests[...] = by_slot.T.reshape(SHARDS, 1, SHARDS)

    pl.semaphore_wait(barrier, SHARDS - 1)

    others = pl.ds(0, SHARDS - 1)
    asked[me] = requests[me]

    @pl.loop(1, SHARDS)
    def _(step):
        d = lax.rem(me + step, SHARDS)
        send(requests.at[d], asked.at[me], send_sems.at[0], recv_sems.at[0], place(d))

    wait(asked.at[others], recv_sems.at[0])
    spread = pltpu.make_async_copy(asked, asked_scalars, load_sems.at[5])
    spread.start()
    loads[0].wait()
    spread.wait()

    def lookup(d):
        for slot in range(CAP):
            stage[slot : slot + 1, :] = table_rows[pl.ds(asked_scalars[d, 0, slot], 1), :]
        return stage[...].astype(bf16)

    @pl.loop(1, SHARDS)
    def _(step):
        d = lax.rem(me + step, SHARDS)
        rows[d] = lookup(d)
        send(rows.at[d], fetched.at[me], send_sems.at[1], recv_sems.at[1], place(d))

    fetched[me] = lookup(me)

    cut = 512
    rank_b, named_qb, named_kb = (v.astype(f32).astype(bf16) for v in (rank, named_q, named_k))
    for c in range(SHARDS * CAP // cut):
        col = lax.broadcasted_iota(jnp.int32, (SHARDS, cut), 1) + c * cut
        dev = lax.broadcasted_iota(jnp.int32, (SHARDS, cut), 0)
        spread_b = (lax.div(col, CAP) == dev).astype(bf16)
        hit = mm(rank_b, spread_b) == lax.rem(col, CAP).astype(f32)
        pick[0:PAIRS, c * cut : (c + 1) * cut] = jnp.where(hit, mm(named_qb, spread_b), 0.0).astype(bf16)
        pick[PAIRS:, c * cut : (c + 1) * cut] = jnp.where(hit, mm(named_kb, spread_b), 0.0).astype(bf16)
        col = lax.broadcasted_iota(jnp.int32, (cut, SHARDS), 0) + c * cut
        dev = lax.broadcasted_iota(jnp.int32, (cut, SHARDS), 1)
        spread_b = (lax.div(col, CAP) == dev).astype(bf16)
        rhs_t = ((1,), (1,))
        hit = mm(spread_b, rank_b, rhs_t) == lax.rem(col, CAP).astype(f32)
        pick_t[c * cut : (c + 1) * cut, 0:PAIRS] = jnp.where(hit, mm(spread_b, named_qb, rhs_t), 0.0).astype(bf16)
        pick_t[c * cut : (c + 1) * cut, PAIRS:] = jnp.where(hit, mm(spread_b, named_kb, rhs_t), 0.0).astype(bf16)

    for load in loads[1:]:
        load.wait()
    wait(rows.at[others], recv_sems.at[1])
    inputs = mm(pick[...], fetched[...].reshape(SHARDS * CAP, WIDTH)).astype(bf16)
    x_in = (inputs[0:PAIRS], inputs[PAIRS:])

    for i in range(2):
        pre = mm(x_in[i], w_in[i])
        pre_act[i] = pre
        hid = (pre * lax.logistic(pre)).astype(bf16)
        hidden[i] = hid
        out = mm(hid, w_out[i])
        out_norm = jnp.sqrt(jnp.sum(out * out, axis=-1, keepdims=True) + 1e-06)
        unit[i] = out / out_norm
        norm[i] = jnp.broadcast_to(out_norm, (PAIRS, WIDTH))
        if i == 0:
            queries[a] = unit[0].astype(bf16)
            for j in range(1, QUERY_PEERS):
                peer = (t, z * QUERY_PEERS + lax.rem(a + j, QUERY_PEERS))
                send(queries.at[a], queries.at[a], send_sems.at[2], recv_sems.at[2], peer)
        else:
            items[z] = unit[1].astype(bf16)
            for j in range(1, ITEM_PEERS):
                peer = (t, lax.rem(z + j, ITEM_PEERS) * QUERY_PEERS + a)
                send(items.at[z], items.at[z], send_sems.at[3], recv_sems.at[3], peer)
    query_unit = queries[a].astype(f32)
    item_unit = items[z].astype(f32)
    wait(items.at[pl.ds(0, ITEM_PEERS - 1)], recv_sems.at[3])
    wait(queries.at[pl.ds(0, QUERY_PEERS - 1)], recv_sems.at[2])

    all_items = items[...].reshape(BLOCK_K, WIDTH)
    sums = []
    for c in range(QUERY_PEERS):
        e = jnp.exp(SCALE * mm(all_items, queries[c], ((1,), (1,))))
        expo[:, c * PAIRS : (c + 1) * PAIRS] = e
        sums.append(jnp.sum(e, axis=0, keepdims=True))
    part_sums[a] = jnp.concatenate(sums, axis=0)
    for j in range(1, QUERY_PEERS):
        peer = (t, z * QUERY_PEERS + lax.rem(a + j, QUERY_PEERS))
        send(part_sums.at[a], part_sums.at[a], send_sems.at[4], recv_sems.at[4], peer)
    own_score = SCALE * jnp.sum(query_unit * item_unit, axis=1, keepdims=True)
    own_score = jnp.sum(jnp.where(lane == row, own_score, 0.0), axis=0, keepdims=True)
    wait(part_sums.at[pl.ds(0, QUERY_PEERS - 1)], recv_sems.at[4])
    total = part_sums[0]
    for c in range(1, QUERY_PEERS):
        total = total + part_sums[c]
    mine = lax.broadcasted_iota(jnp.int32, (QUERY_PEERS, PAIRS), 0) == a
    own_total = jnp.sum(jnp.where(mine, total, 0.0), axis=0, keepdims=True)
    loss_ref[...] = jnp.log(own_total) - own_score
    inverse = 1.0 / total
    for c in range(QUERY_PEERS):
        at = slice(c * PAIRS, (c + 1) * PAIRS)
        soft[:, at] = (expo[:, at] * inverse[c : c + 1, :]).astype(bf16)

    def part_q(c):
        block = soft[:, pl.ds(pl.multiple_of(c * PAIRS, PAIRS), PAIRS)]
        return mm(block, all_items, ((0,), (0,)))

    def part_k(c):
        block = soft[pl.ds(pl.multiple_of(c * PAIRS, PAIRS), PAIRS), :]
        return mm(block, queries[...].reshape(BLOCK_Q, WIDTH))

    for j in range(1, QUERY_PEERS):
        c = lax.rem(a + j, QUERY_PEERS)
        q_send[j - 1] = part_q(c).astype(bf16)
        send(q_send.at[j - 1], q_recv.at[j - 1], send_sems.at[5], recv_sems.at[5], (t, z * QUERY_PEERS + c))
    for j in range(1, ITEM_PEERS):
        c = lax.rem(z + j, ITEM_PEERS)
        k_send[j - 1] = part_k(c).astype(bf16)
        send(k_send.at[j - 1], k_recv.at[j - 1], send_sems.at[6], recv_sems.at[6], (t, c * QUERY_PEERS + a))
    grad_q = part_q(a) - item_unit
    grad_k = part_k(z) - query_unit
    wait(q_recv, recv_sems.at[5])
    for j in range(QUERY_PEERS - 1):
        grad_q = grad_q + q_recv[j].astype(f32)
    wait(k_recv, recv_sems.at[6])
    for j in range(ITEM_PEERS - 1):
        grad_k = grad_k + k_recv[j].astype(f32)

    grad_out, grad_pre, grad_x = [], [], []
    for i, grad_unit in enumerate((SCALE * grad_q, SCALE * grad_k)):
        u = unit[i]
        g = ((grad_unit - u * jnp.sum(grad_unit * u, axis=-1, keepdims=True)) / norm[i]).astype(bf16)
        grad_hidden = mm(g, w_out[i], ((1,), (1,)))
        pre = pre_act[i]
        s = lax.logistic(pre)
        gp = (grad_hidden * s * (1.0 + pre * (1.0 - s))).astype(bf16)
        grad_out.append(g)
        grad_pre.append(gp)
        grad_x.append(mm(gp, w_in[i], ((1,), (1,))).astype(bf16))

    slots[...] = (
        mm(pick_t[...], jnp.concatenate(grad_x, axis=0)).astype(bf16).reshape(SHARDS, CAP, WIDTH)
    )

    @pl.loop(1, SHARDS)
    def _(step):
        d = lax.rem(me + step, SHARDS)
        send(slots.at[d], returned.at[me], send_sems.at[7], recv_sems.at[7], place(d))

    returned[me] = slots[me]

    for i in range(2):
        base = i * HALF
        for c in range(0, HIDDEN, WIDTH):
            grads[base + c : base + c + WIDTH] = mm(
                x_in[i], grad_pre[i][:, c : c + WIDTH], ((0,), (0,))
            ).astype(bf16)
        base += HIDDEN
        for c in range(0, HIDDEN, WIDTH):
            grads[base + c : base + c + WIDTH] = mm(
                hidden[i, :, c : c + WIDTH], grad_out[i], ((0,), (0,))
            ).astype(bf16)

    def half_at(c):
        return pl.ds(pl.multiple_of(c * HALF, HALF), HALF)

    send(grads.at[half_at(1 - core)], core_recv, send_sems.at[8], recv_sems.at[8], chip(coords, 1 - core))
    wait(core_recv, recv_sems.at[8])
    half[...] = (grads[half_at(core)].astype(f32) + core_recv[...].astype(f32)).astype(bf16)

    def along(axis, j):
        moved = list(coords)
        moved[axis] = lax.rem(coords[axis] + j, 4)
        return moved[axis], chip(moved, core)

    def rows_at(start, size):
        return pl.ds(pl.multiple_of(start, 16), size)

    at1, at2 = 0, 0
    spans = []
    for base, size, _ in PARTS:
        spans.append((at1, at2))
        at1, at2 = at1 + size // 4, at2 + size // 16
    for p, (base, size, axes) in enumerate(PARTS):
        n = size // 4
        for j in range(1, 4):
            c, device = along(axes[0], j)
            send(half.at[rows_at(base + c * n, n)], recv1.at[j - 1, pl.ds(spans[p][0], n)],
                 ring_send.at[p, 0], ring_recv.at[p, 0], device)
    for p, (base, size, axes) in enumerate(PARTS):
        n, m = size // 4, size // 16
        at = pl.ds(spans[p][0], n)
        wait(recv1.at[:, at], ring_recv.at[p, 0])
        total1 = half[rows_at(base + coords[axes[0]] * n, n)].astype(f32)
        for j in range(3):
            total1 = total1 + recv1[j, at].astype(f32)
        sum1[at] = total1.astype(bf16)
        for j in range(1, 4):
            c, device = along(axes[1], j)
            send(sum1.at[rows_at(spans[p][0] + c * m, m)], recv2.at[j - 1, pl.ds(spans[p][1], m)],
                 ring_send.at[p, 1], ring_recv.at[p, 1], device)
    for p, (base, size, axes) in enumerate(PARTS):
        m = size // 16
        at = pl.ds(spans[p][1], m)
        wait(recv2.at[:, at], ring_recv.at[p, 1])
        total2 = sum1[rows_at(spans[p][0] + coords[axes[1]] * m, m)].astype(f32)
        for j in range(3):
            total2 = total2 + recv2[j, at].astype(f32)
        c3 = coords[axes[2]]
        recv3[c3, at] = total2.astype(bf16)
        for j in range(1, 4):
            _, device = along(axes[2], j)
            send(recv3.at[c3, at], recv3.at[c3, at], ring_send.at[p, 2], ring_recv.at[p, 2], device)
    for p, (base, size, axes) in enumerate(PARTS):
        n, m = size // 4, size // 16
        at = pl.ds(spans[p][1], m)
        wait(recv3.at[pl.ds(0, 3), at], ring_recv.at[p, 2])
        total3 = recv3[0, at].astype(f32)
        for j in range(1, 4):
            total3 = total3 + recv3[j, at].astype(f32)
        mine = rows_at(core * HALF + base + coords[axes[0]] * n + coords[axes[1]] * m, m)
        summed[mine] = total3.astype(bf16)
        for j in range(1, 4):
            _, device = along(axes[1], j)
            send(summed.at[mine], summed.at[mine], ring_send.at[p, 3], ring_recv.at[p, 3], device)
    for p, (base, size, axes) in enumerate(PARTS):
        n, m = size // 4, size // 16
        wait(summed.at[pl.ds(0, 3 * m)], ring_recv.at[p, 3])
        mine = rows_at(core * HALF + base + coords[axes[0]] * n, n)
        for j in range(1, 4):
            _, device = along(axes[0], j)
            send(summed.at[mine], summed.at[mine], ring_send.at[p, 4], ring_recv.at[p, 4], device)
    for p, (base, size, axes) in enumerate(PARTS):
        n = size // 4
        wait(summed.at[pl.ds(0, 3 * n)], ring_recv.at[p, 4])
        mine = rows_at(core * HALF + base, size)
        send(summed.at[mine], summed.at[mine], ring_send.at[p, 5], ring_recv.at[p, 5], chip(coords, 1 - core))
    for p, (base, size, axes) in enumerate(PARTS):
        wait(summed.at[pl.ds(0, size)], ring_recv.at[p, 5])

    wait(rows.at[others], recv_sems.at[7])
    for ref, i in (
        (requests.at[others], 0),
        (rows.at[others], 1),
        (queries.at[pl.ds(0, QUERY_PEERS - 1)], 2),
        (items.at[pl.ds(0, ITEM_PEERS - 1)], 3),
        (part_sums.at[pl.ds(0, QUERY_PEERS - 1)], 4),
        (q_send, 5),
        (k_send, 6),
        (slots.at[others], 7),
        (core_recv, 8),
    ):
        wait(ref, send_sems.at[i])
    for p, (base, size, axes) in enumerate(PARTS):
        n, m = size // 4, size // 16
        for i, count in enumerate((3 * n, 3 * m, 3 * m, 3 * m, 3 * n, size)):
            wait(summed.at[pl.ds(0, count)], ring_send.at[p, i])


def train_step(owner, offset, table, query_in, query_out, item_in, item_out):
    rows1 = sum(size // 4 for _, size, _ in PARTS)
    rows2 = sum(size // 16 for _, size, _ in PARTS)
    vmem = pl.BlockSpec(memory_space=pltpu.VMEM)
    hbm = pl.BlockSpec(memory_space=pl.ANY)
    V = pltpu.VMEM
    return pl.pallas_call(
        step_kernel,
        out_shape=(
            jax.ShapeDtypeStruct((1, PAIRS), f32),
            jax.ShapeDtypeStruct((SHARDS, 1, SHARDS), jnp.int32),
            jax.ShapeDtypeStruct((SHARDS, CAP, WIDTH), bf16),
            jax.ShapeDtypeStruct((GRAD_ROWS, WIDTH), bf16),
        ),
        in_specs=[vmem, vmem, hbm, hbm, hbm, hbm, hbm],
        out_specs=(vmem,) * 4,
        scratch_shapes=[
            V((ROWS, WIDTH), f32),
            V((2, WIDTH, HIDDEN), bf16),
            V((2, HIDDEN, WIDTH), bf16),
            V((SHARDS, 1, SHARDS), jnp.int32),
            pltpu.SMEM((SHARDS, 1, SHARDS), jnp.int32),
            V((CAP, WIDTH), f32),
            V((SHARDS, CAP, WIDTH), bf16),
            V((SHARDS, CAP, WIDTH), bf16),
            V((2 * PAIRS, SHARDS * CAP), bf16),
            V((SHARDS * CAP, 2 * PAIRS), bf16),
            V((2, PAIRS, HIDDEN), f32),
            V((2, PAIRS, HIDDEN), bf16),
            V((2, PAIRS, WIDTH), f32),
            V((2, PAIRS, WIDTH), f32),
            V((QUERY_PEERS, PAIRS, WIDTH), bf16),
            V((ITEM_PEERS, PAIRS, WIDTH), bf16),
            V((BLOCK_K, BLOCK_Q), f32),
            V((BLOCK_K, BLOCK_Q), bf16),
            V((QUERY_PEERS, QUERY_PEERS, PAIRS), f32),
            V((QUERY_PEERS - 1, PAIRS, WIDTH), bf16),
            V((QUERY_PEERS - 1, PAIRS, WIDTH), bf16),
            V((ITEM_PEERS - 1, PAIRS, WIDTH), bf16),
            V((ITEM_PEERS - 1, PAIRS, WIDTH), bf16),
            V((SHARDS, CAP, WIDTH), bf16),
            V((GRAD_ROWS, WIDTH), bf16),
            V((HALF, WIDTH), bf16),
            V((HALF, WIDTH), bf16),
            V((rows1, WIDTH), bf16),
            V((3, rows1, WIDTH), bf16),
            V((3, rows2, WIDTH), bf16),
            V((4, rows2, WIDTH), bf16),
            pltpu.SemaphoreType.DMA((6,)),
            pltpu.SemaphoreType.DMA((9,)),
            pltpu.SemaphoreType.DMA((9,)),
            pltpu.SemaphoreType.DMA((len(PARTS), 6)),
            pltpu.SemaphoreType.DMA((len(PARTS), 6)),
        ],
        compiler_params=pltpu.CompilerParams(
            collective_id=0, has_side_effects=True, vmem_limit_bytes=56 << 20
        ),
    )(owner, offset, table, query_in, query_out, item_in, item_out)


def update_kernel(
    asked, returned, summed, table_grad, q_in, q_out, k_in, k_out,
    total, wide_in, wide_out, stage, sems,
):
    copies = []
    for i, (out_in, out_out) in enumerate(((q_in, q_out), (k_in, k_out))):
        base = i * HALF
        for c in range(0, HIDDEN, WIDTH):
            wide_in[i, :, c : c + WIDTH] = summed[base + c : base + c + WIDTH].astype(f32)
        wide_out[i] = summed[base + HIDDEN : base + HALF].astype(f32)
        copies.append(pltpu.make_async_copy(wide_in.at[i], out_in, sems.at[2 * i]))
        copies.append(pltpu.make_async_copy(wide_out.at[i], out_out, sems.at[2 * i + 1]))
        copies[-2].start()
        copies[-1].start()

    @pl.loop(0, ROWS, step=256)
    def _(r):
        total[pl.ds(r, 256), :] = jnp.zeros((256, WIDTH), f32)

    @pl.loop(0, SHARDS)
    def _(d):
        stage[...] = returned[d].astype(f32)
        for slot in range(CAP):
            at = pl.ds(asked[d, 0, slot], 1)
            total[at, :] += stage[slot : slot + 1, :]

    last = pltpu.make_async_copy(total, table_grad, sems.at[4])
    last.start()
    for copy in copies:
        copy.wait()
    last.wait()


def update(asked, returned, summed):
    vmem = pl.BlockSpec(memory_space=pltpu.VMEM)
    hbm = pl.BlockSpec(memory_space=pl.ANY)
    in_shape = jax.ShapeDtypeStruct((WIDTH, HIDDEN), f32)
    out_shape = jax.ShapeDtypeStruct((HIDDEN, WIDTH), f32)
    return pl.pallas_call(
        update_kernel,
        out_shape=(jax.ShapeDtypeStruct((ROWS, WIDTH), f32), in_shape, out_shape, in_shape, out_shape),
        in_specs=[pl.BlockSpec(memory_space=pltpu.SMEM), vmem, vmem],
        out_specs=(hbm,) * 5,
        scratch_shapes=[
            pltpu.VMEM((ROWS, WIDTH), f32),
            pltpu.VMEM((2, WIDTH, HIDDEN), f32),
            pltpu.VMEM((2, HIDDEN, WIDTH), f32),
            pltpu.VMEM((CAP, WIDTH), f32),
            pltpu.SemaphoreType.DMA((5,)),
        ],
        compiler_params=pltpu.CompilerParams(vmem_limit_bytes=40 << 20),
    )(asked, returned, summed)


def local(table, feature_owner, feature_offset, query_in, query_out, item_in, item_out):
    loss, asked, returned, summed = train_step(
        feature_owner, feature_offset, table, query_in, query_out, item_in, item_out
    )
    table_grad, q_in, q_out, k_in, k_out = update(asked, returned, summed)
    return (loss.reshape(PAIRS), table_grad, q_in, q_out, k_in, k_out)


def solution(mesh):
    in_specs = (
        P(("table", "dp"), None),
        P(("table", "dp"), None),
        P(("table", "dp"), None),
        P(),
        P(),
        P(),
        P(),
    )
    out_specs = (P(("table", "dp")), P(("table", "dp"), None), P(), P(), P(), P())
    return jax.shard_map(local, mesh=mesh, in_specs=in_specs, out_specs=out_specs, check_vma=False)
```

time: 516 us -> 127 us (0.25)
  the two profiles are of different devices: /device:TPU:1 before, /device:TPU:25 now
where the time goes in v2:
time: 127 us
  Pallas kernels  118 us (93%)
  local copies, waits for them, and re-layouts  7.61 us (6%)
    pallas_call x1, Pallas kernels, train_step(): pl.pallas_call(step_kernel, out_shape=(jax.ShapeDtypeStruct((1, PAIRS), f...  99.3 us
    pallas_call x1, Pallas kernels, update(): pl.pallas_call(update_kernel, out_shape=(jax.ShapeDtypeStruct((ROWS, WIDT...  18.9 us
    unnamed x9, local copies, waits for them, and re-layouts  7.61 us

profile of v2, /device:TPU:25, one launch (start us, length us, event | category | flops | bytes accessed | tf_op | source)
XLA Modules:
  0.0 126.5 jit_solution(14293499870270381839)
XLA Ops:
  0.6 1.4 %copy.13.owner_ref = s32[128,8]{1,0:T(8,128)} copy(s32[128,8]{0,1:T(8,128)} %param.8) | data formatting | bytes 8192 | tf_op args[1]
  2.0 1.4 %copy.14.offset_ref = s32[128,8]{1,0:T(8,128)} copy(s32[128,8]{0,1:T(8,128)} %param.9) | data formatting | bytes 8192 | tf_op args[2]
  3.5 99.3 %shard_map.118 = (f32[1,128]{1,0:T(1,128)}, s32[128,1,128]{2,1,0:T(1,128)}, bf16[128,16,256]{2,1,0:T(8,128)(2,1)}, bf16[4096,256]{1,0:T(8,128)(2,1)}) custom-call(s32[128,8]{1,0:T(8,128)} %copy.13.owner_ref, s32[128,8]{1,0:T(8,128)} %copy.14.offset_ref, f32[8192,256]{1,0:T(8,128)} %table_ref.1, bf16[256,1024]{1,0:T(8,128)(2,1)} %w_ins_ref.1, ...), custom_call_target="tpu_custom_call" | custom-call | tf_op jit(solution)/shard_map/pallas_call | solution.py:369
  102.8 0.0 copy-start
  102.8 1.6 %copy-done = bf16[4096,256]{1,0:T(8,128)(2,1)S(1)} copy-done((bf16[4096,256]{1,0:T(8,128)(2,1)S(1)}, bf16[4096,256]{1,0:T(8,128)(2,1)}, u32[]{:S(2)}) %copy-start) | copy-done | bytes 2097176
  104.4 0.0 copy-start.1
  104.4 1.2 copy-done.1
  105.6 0.0 copy-start.2
  105.6 0.8 copy-done.2
  106.5 18.9 %shard_map.119 = (f32[8192,256]{1,0:T(8,128)}, f32[256,1024]{1,0:T(8,128)}, f32[1024,256]{1,0:T(8,128)}, f32[256,1024]{1,0:T(8,128)}, f32[1024,256]{1,0:T(8,128)}) custom-call(s32[128,1,128]{2,1,0:T(1,128)S(1)} %copy-done.2, bf16[128,16,256]{2,1,0:T(8,128)(2,1)S(1)} %copy-done.1, bf16[4096,256]{1,0:T(8,128)(2,1)S(1)} %copy-done), custom_call_target="tpu_custom_call" | custom-call | tf_op jit(solution)/shard_map/pallas_call | solution.py:461
  125.4 1.1 copy.16
Async XLA Ops:
  102.8 1.6 %copy-start = (bf16[4096,256]{1,0:T(8,128)(2,1)S(1)}, bf16[4096,256]{1,0:T(8,128)(2,1)}, u32[]{:S(2)}) copy-start(bf16[4096,256]{1,0:T(8,128)(2,1)} %get-tuple-element.18.summed) | copy-start | bytes 6291460
  104.4 1.2 copy-start.1
  105.6 0.8 copy-start.2

commit v3 on v2

--- a/solution.py
+++ b/solution.py
@@ -21,6 +21,7 @@
 GRAD_ROWS = 4 * HIDDEN
 HALF = GRAD_ROWS // 2
 PARTS = ((0, 768, (0, 1, 2)), (768, 768, (2, 0, 1)), (1536, 512, (1, 2, 0)))
+CUTS = (32, 64, 96)
 f32 = jnp.float32
 bf16 = jnp.bfloat16
 
@@ -34,7 +35,7 @@
     loss_ref, asked, returned, summed,
     table_rows, w_in, w_out, requests, asked_scalars, stage, rows, fetched, pick, pick_t,
     pre_act, hidden, unit, norm, queries, items, expo, soft, part_sums,
-    q_send, q_recv, k_send, k_recv, slots, grads, core_recv, half, sum1, recv1, recv2, recv3,
+    q_send, q_recv, k_send, k_recv, slots, inputs, grad_out, grad_pre, core_send, core_recv, half, sum1, recv1, recv2, recv3,
     load_sems, send_sems, recv_sems, ring_send, ring_recv,
 ):
     t = lax.axis_index("table")
@@ -87,8 +88,11 @@
 
     lane = lax.broadcasted_iota(jnp.int32, (PAIRS, SHARDS), 1)
     row = lax.broadcasted_iota(jnp.int32, (PAIRS, SHARDS), 0)
-    names = [(owner_ref[:, k : k + 1] == lane).astype(jnp.int32) for k in range(8)]
-    offsets = sum(names[k] * offset_ref[:, k : k + 1] for k in range(8))
+    below = jnp.zeros((SHARDS - 8, PAIRS), jnp.int32)
+    owner = jnp.concatenate([owner_ref[...], below], axis=0).T
+    offset = jnp.concatenate([offset_ref[...], below], axis=0).T
+    names = [(owner[:, k : k + 1] == lane).astype(jnp.int32) for k in range(8)]
+    offsets = sum(names[k] * offset[:, k : k + 1] for k in range(8))
     named_q = sum(names[:4])
     named_k = sum(names[4:])
     named = named_q + named_k
@@ -153,11 +157,12 @@
     for load in loads[1:]:
         load.wait()
     wait(rows.at[others], recv_sems.at[1])
-    inputs = mm(pick[...], fetched[...].reshape(SHARDS * CAP, WIDTH)).astype(bf16)
-    x_in = (inputs[0:PAIRS], inputs[PAIRS:])
+    inputs[...] = (
+        mm(pick[...], fetched[...].reshape(SHARDS * CAP, WIDTH)).astype(bf16).reshape(2, PAIRS, WIDTH)
+    )
 
     for i in range(2):
-        pre = mm(x_in[i], w_in[i])
+        pre = mm(inputs[i], w_in[i])
         pre_act[i] = pre
         hid = (pre * lax.logistic(pre)).astype(bf16)
         hidden[i] = hid
@@ -185,13 +190,25 @@
     for c in range(QUERY_PEERS):
         e = jnp.exp(SCALE * mm(all_items, queries[c], ((1,), (1,))))
         expo[:, c * PAIRS : (c + 1) * PAIRS] = e
+        soft[:, c * PAIRS : (c + 1) * PAIRS] = e.astype(bf16)
         sums.append(jnp.sum(e, axis=0, keepdims=True))
     part_sums[a] = jnp.concatenate(sums, axis=0)
     for j in range(1, QUERY_PEERS):
         peer = (t, z * QUERY_PEERS + lax.rem(a + j, QUERY_PEERS))
         send(part_sums.at[a], part_sums.at[a], send_sems.at[4], recv_sems.at[4], peer)
+
+    def part_q(c):
+        block = soft[:, pl.ds(pl.multiple_of(c * PAIRS, PAIRS), PAIRS)]
+        return mm(block, all_items, ((0,), (0,)))
+
+    for j in range(1, QUERY_PEERS):
+        c = lax.rem(a + j, QUERY_PEERS)
+        q_send[j - 1] = part_q(c).astype(bf16)
+        send(q_send.at[j - 1], q_recv.at[j - 1], send_sems.at[5], recv_sems.at[5], (t, z * QUERY_PEERS + c))
+    grad_q = part_q(a)
     own_score = SCALE * jnp.sum(query_unit * item_unit, axis=1, keepdims=True)
     own_score = jnp.sum(jnp.where(lane == row, own_score, 0.0), axis=0, keepdims=True)
+
     wait(part_sums.at[pl.ds(0, QUERY_PEERS - 1)], recv_sems.at[4])
     total = part_sums[0]
     for c in range(1, QUERY_PEERS):
@@ -200,36 +217,29 @@
     own_total = jnp.sum(jnp.where(mine, total, 0.0), axis=0, keepdims=True)
     loss_ref[...] = jnp.log(own_total) - own_score
     inverse = 1.0 / total
+    own_inverse = jnp.sum(jnp.where(lane == row, 1.0 / own_total, 0.0), axis=1, keepdims=True)
     for c in range(QUERY_PEERS):
         at = slice(c * PAIRS, (c + 1) * PAIRS)
         soft[:, at] = (expo[:, at] * inverse[c : c + 1, :]).astype(bf16)
 
-    def part_q(c):
-        block = soft[:, pl.ds(pl.multiple_of(c * PAIRS, PAIRS), PAIRS)]
-        return mm(block, all_items, ((0,), (0,)))
-
     def part_k(c):
         block = soft[pl.ds(pl.multiple_of(c * PAIRS, PAIRS), PAIRS), :]
         return mm(block, queries[...].reshape(BLOCK_Q, WIDTH))
 
-    for j in range(1, QUERY_PEERS):
-        c = lax.rem(a + j, QUERY_PEERS)
-        q_send[j - 1] = part_q(c).astype(bf16)
-        send(q_send.at[j - 1], q_recv.at[j - 1], send_sems.at[5], recv_sems.at[5], (t, z * QUERY_PEERS + c))
     for j in range(1, ITEM_PEERS):
         c = lax.rem(z + j, ITEM_PEERS)
         k_send[j - 1] = part_k(c).astype(bf16)
         send(k_send.at[j - 1], k_recv.at[j - 1], send_sems.at[6], recv_sems.at[6], (t, c * QUERY_PEERS + a))
-    grad_q = part_q(a) - item_unit
     grad_k = part_k(z) - query_unit
     wait(q_recv, recv_sems.at[5])
     for j in range(QUERY_PEERS - 1):
         grad_q = grad_q + q_recv[j].astype(f32)
+    grad_q = grad_q * own_inverse - item_unit
     wait(k_recv, recv_sems.at[6])
     for j in range(ITEM_PEERS - 1):
         grad_k = grad_k + k_recv[j].astype(f32)
 
-    grad_out, grad_pre, grad_x = [], [], []
+    grad_x = []
     for i, grad_unit in enumerate((SCALE * grad_q, SCALE * grad_k)):
         u = unit[i]
         g = ((grad_unit - u * jnp.sum(grad_unit * u, axis=-1, keepdims=True)) / norm[i]).astype(bf16)
@@ -237,39 +247,34 @@
         pre = pre_act[i]
         s = lax.logistic(pre)
         gp = (grad_hidden * s * (1.0 + pre * (1.0 - s))).astype(bf16)
-        grad_out.append(g)
-        grad_pre.append(gp)
+        grad_out[i] = g
+        grad_pre[i] = gp
         grad_x.append(mm(gp, w_in[i], ((1,), (1,))).astype(bf16))
+
+    def tower_rows(i, block):
+        at = slice(block % 4 * WIDTH, (block % 4 + 1) * WIDTH)
+        if block < 4:
+            return mm(inputs[i], grad_pre[i, :, at], ((0,), (0,)))
+        return mm(hidden[i, :, at], grad_out[i], ((0,), (0,)))
+
+    for p, (base, size, axes) in enumerate(PARTS):
+        for r in range(base, base + size, WIDTH):
+            core_send[r : r + WIDTH] = tower_rows(1 - core, r // WIDTH).astype(bf16)
+        at = pl.ds(base, size)
+        send(core_send.at[at], core_recv.at[at], ring_send.at[p, 0], ring_recv.at[p, 0], chip(coords, 1 - core))
 
     slots[...] = (
         mm(pick_t[...], jnp.concatenate(grad_x, axis=0)).astype(bf16).reshape(SHARDS, CAP, WIDTH)
     )
 
-    @pl.loop(1, SHARDS)
-    def _(step):
-        d = lax.rem(me + step, SHARDS)
-        send(slots.at[d], returned.at[me], send_sems.at[7], recv_sems.at[7], place(d))
-
+    def send_slots(first, last):
+        @pl.loop(first, last)
+        def _(step):
+            d = lax.rem(me + step, SHARDS)
+            send(slots.at[d], returned.at[me], send_sems.at[7], recv_sems.at[7], place(d))
+
+    send_slots(1, CUTS[0])
     returned[me] = slots[me]
-
-    for i in range(2):
-        base = i * HALF
-        for c in range(0, HIDDEN, WIDTH):
-            grads[base + c : base + c + WIDTH] = mm(
-                x_in[i], grad_pre[i][:, c : c + WIDTH], ((0,), (0,))
-            ).astype(bf16)
-        base += HIDDEN
-        for c in range(0, HIDDEN, WIDTH):
-            grads[base + c : base + c + WIDTH] = mm(
-                hidden[i, :, c : c + WIDTH], grad_out[i], ((0,), (0,))
-            ).astype(bf16)
-
-    def half_at(c):
-        return pl.ds(pl.multiple_of(c * HALF, HALF), HALF)
-
-    send(grads.at[half_at(1 - core)], core_recv, send_sems.at[8], recv_sems.at[8], chip(coords, 1 - core))
-    wait(core_recv, recv_sems.at[8])
-    half[...] = (grads[half_at(core)].astype(f32) + core_recv[...].astype(f32)).astype(bf16)
 
     def along(axis, j):
         moved = list(coords)
@@ -286,14 +291,19 @@
         at1, at2 = at1 + size // 4, at2 + size // 16
     for p, (base, size, axes) in enumerate(PARTS):
         n = size // 4
+        wait(core_recv.at[pl.ds(base, size)], ring_recv.at[p, 0])
+        for r in range(base, base + size, WIDTH):
+            at = slice(r, r + WIDTH)
+            half[at] = (tower_rows(core, r // WIDTH) + core_recv[at].astype(f32)).astype(bf16)
         for j in range(1, 4):
             c, device = along(axes[0], j)
             send(half.at[rows_at(base + c * n, n)], recv1.at[j - 1, pl.ds(spans[p][0], n)],
-                 ring_send.at[p, 0], ring_recv.at[p, 0], device)
+                 ring_send.at[p, 1], ring_recv.at[p, 1], device)
+    send_slots(CUTS[0], CUTS[1])
     for p, (base, size, axes) in enumerate(PARTS):
         n, m = size // 4, size // 16
         at = pl.ds(spans[p][0], n)
-        wait(recv1.at[:, at], ring_recv.at[p, 0])
+        wait(recv1.at[:, at], ring_recv.at[p, 1])
         total1 = half[rows_at(base + coords[axes[0]] * n, n)].astype(f32)
         for j in range(3):
             total1 = total1 + recv1[j, at].astype(f32)
@@ -301,11 +311,12 @@
         for j in range(1, 4):
             c, device = along(axes[1], j)
             send(sum1.at[rows_at(spans[p][0] + c * m, m)], recv2.at[j - 1, pl.ds(spans[p][1], m)],
-                 ring_send.at[p, 1], ring_recv.at[p, 1], device)
+                 ring_send.at[p, 2], ring_recv.at[p, 2], device)
+    send_slots(CUTS[1], CUTS[2])
     for p, (base, size, axes) in enumerate(PARTS):
         m = size // 16
         at = pl.ds(spans[p][1], m)
-        wait(recv2.at[:, at], ring_recv.at[p, 1])
+        wait(recv2.at[:, at], ring_recv.at[p, 2])
         total2 = sum1[rows_at(spans[p][0] + coords[axes[1]] * m, m)].astype(f32)
         for j in range(3):
             total2 = total2 + recv2[j, at].astype(f32)
@@ -313,11 +324,12 @@
         recv3[c3, at] = total2.astype(bf16)
         for j in range(1, 4):
             _, device = along(axes[2], j)
-            send(recv3.at[c3, at], recv3.at[c3, at], ring_send.at[p, 2], ring_recv.at[p, 2], device)
+            send(recv3.at[c3, at], recv3.at[c3, at], ring_send.at[p, 3], ring_recv.at[p, 3], device)
+    send_slots(CUTS[2], SHARDS)
     for p, (base, size, axes) in enumerate(PARTS):
         n, m = size // 4, size // 16
         at = pl.ds(spans[p][1], m)
-        wait(recv3.at[pl.ds(0, 3), at], ring_recv.at[p, 2])
+        wait(recv3.at[pl.ds(0, 3), at], ring_recv.at[p, 3])
         total3 = recv3[0, at].astype(f32)
         for j in range(1, 4):
             total3 = total3 + recv3[j, at].astype(f32)
@@ -325,21 +337,23 @@
         summed[mine] = total3.astype(bf16)
         for j in range(1, 4):
             _, device = along(axes[1], j)
-            send(summed.at[mine], summed.at[mine], ring_send.at[p, 3], ring_recv.at[p, 3], device)
+            send(summed.at[mine], summed.at[mine], ring_send.at[p, 4], ring_recv.at[p, 4], device)
     for p, (base, size, axes) in enumerate(PARTS):
         n, m = size // 4, size // 16
-        wait(summed.at[pl.ds(0, 3 * m)], ring_recv.at[p, 3])
+        wait(summed.at[pl.ds(0, 3 * m)], ring_recv.at[p, 4])
         mine = rows_at(core * HALF + base + coords[axes[0]] * n, n)
         for j in range(1, 4):
             _, device = along(axes[0], j)
-            send(summed.at[mine], summed.at[mine], ring_send.at[p, 4], ring_recv.at[p, 4], device)
-    for p, (base, size, axes) in enumerate(PARTS):
-        n = size // 4
-        wait(summed.at[pl.ds(0, 3 * n)], ring_recv.at[p, 4])
-        mine = rows_at(core * HALF + base, size)
-        send(summed.at[mine], summed.at[mine], ring_send.at[p, 5], ring_recv.at[p, 5], chip(coords, 1 - core))
-    for p, (base, size, axes) in enumerate(PARTS):
-        wait(summed.at[pl.ds(0, size)], ring_recv.at[p, 5])
+            send(summed.at[mine], summed.at[mine], ring_send.at[p, 4 + j], ring_recv.at[p, 4 + j], device)
+        send(summed.at[mine], summed.at[mine], ring_send.at[p, 8], ring_recv.at[p, 8], chip(coords, 1 - core))
+    for j in (1, 3, 2):
+        for p, (base, size, axes) in enumerate(PARTS):
+            n = size // 4
+            wait(summed.at[pl.ds(0, n)], ring_recv.at[p, 4 + j])
+            there = rows_at(core * HALF + base + lax.rem(coords[axes[0]] + 4 - j, 4) * n, n)
+            send(summed.at[there], summed.at[there], ring_send.at[p, 8], ring_recv.at[p, 8], chip(coords, 1 - core))
+    for p, (base, size, axes) in enumerate(PARTS):
+        wait(summed.at[pl.ds(0, size)], ring_recv.at[p, 8])
 
     wait(rows.at[others], recv_sems.at[7])
     for ref, i in (
@@ -351,12 +365,11 @@
         (q_send, 5),
         (k_send, 6),
         (slots.at[others], 7),
-        (core_recv, 8),
     ):
         wait(ref, send_sems.at[i])
     for p, (base, size, axes) in enumerate(PARTS):
         n, m = size // 4, size // 16
-        for i, count in enumerate((3 * n, 3 * m, 3 * m, 3 * m, 3 * n, size)):
+        for i, count in enumerate((size, 3 * n, 3 * m, 3 * m, 3 * m, n, n, n, size)):
             wait(summed.at[pl.ds(0, count)], ring_send.at[p, i])
 
 
@@ -401,7 +414,10 @@
             V((ITEM_PEERS - 1, PAIRS, WIDTH), bf16),
             V((ITEM_PEERS - 1, PAIRS, WIDTH), bf16),
             V((SHARDS, CAP, WIDTH), bf16),
-            V((GRAD_ROWS, WIDTH), bf16),
+            V((2, PAIRS, WIDTH), bf16),
+            V((2, PAIRS, WIDTH), bf16),
+            V((2, PAIRS, HIDDEN), bf16),
+            V((HALF, WIDTH), bf16),
             V((HALF, WIDTH), bf16),
             V((HALF, WIDTH), bf16),
             V((rows1, WIDTH), bf16),
@@ -409,10 +425,10 @@
             V((3, rows2, WIDTH), bf16),
             V((4, rows2, WIDTH), bf16),
             pltpu.SemaphoreType.DMA((6,)),
-            pltpu.SemaphoreType.DMA((9,)),
-            pltpu.SemaphoreType.DMA((9,)),
-            pltpu.SemaphoreType.DMA((len(PARTS), 6)),
-            pltpu.SemaphoreType.DMA((len(PARTS), 6)),
+            pltpu.SemaphoreType.DMA((8,)),
+            pltpu.SemaphoreType.DMA((8,)),
+            pltpu.SemaphoreType.DMA((len(PARTS), 9)),
+            pltpu.SemaphoreType.DMA((len(PARTS), 9)),
         ],
         compiler_params=pltpu.CompilerParams(
             collective_id=0, has_side_effects=True, vmem_limit_bytes=56 << 20
@@ -421,64 +437,99 @@
 
 
 def update_kernel(
-    asked, returned, summed, table_grad, q_in, q_out, k_in, k_out,
-    total, wide_in, wide_out, stage, sems,
+    asked_ref, returned_ref, summed_ref, loss_ref,
+    table_grad, q_in, q_out, k_in, k_out, loss_out,
+    asked, returned, summed, total, other, wide_in, wide_out, stage, sems,
 ):
+    loads = [
+        pltpu.make_async_copy(src, dst, sems.at[i])
+        for i, (src, dst) in enumerate(
+            [(summed_ref, summed), (asked_ref, asked), (returned_ref, returned)]
+        )
+    ]
+    for load in loads:
+        load.start()
+    loss_out[...] = loss_ref[...]
+
+    @pl.loop(0, ROWS, step=256)
+    def _(r):
+        total[pl.ds(r, 256), :] = jnp.zeros((256, WIDTH), f32)
+        other[pl.ds(r, 256), :] = jnp.zeros((256, WIDTH), f32)
+
+    loads[0].wait()
     copies = []
     for i, (out_in, out_out) in enumerate(((q_in, q_out), (k_in, k_out))):
         base = i * HALF
         for c in range(0, HIDDEN, WIDTH):
             wide_in[i, :, c : c + WIDTH] = summed[base + c : base + c + WIDTH].astype(f32)
         wide_out[i] = summed[base + HIDDEN : base + HALF].astype(f32)
-        copies.append(pltpu.make_async_copy(wide_in.at[i], out_in, sems.at[2 * i]))
-        copies.append(pltpu.make_async_copy(wide_out.at[i], out_out, sems.at[2 * i + 1]))
+        copies.append(pltpu.make_async_copy(wide_in.at[i], out_in, sems.at[3 + 2 * i]))
+        copies.append(pltpu.make_async_copy(wide_out.at[i], out_out, sems.at[4 + 2 * i]))
         copies[-2].start()
         copies[-1].start()
-
-    @pl.loop(0, ROWS, step=256)
-    def _(r):
-        total[pl.ds(r, 256), :] = jnp.zeros((256, WIDTH), f32)
+    loads[1].wait()
+    loads[2].wait()
 
     @pl.loop(0, SHARDS)
     def _(d):
         stage[...] = returned[d].astype(f32)
-        for slot in range(CAP):
-            at = pl.ds(asked[d, 0, slot], 1)
-            total[at, :] += stage[slot : slot + 1, :]
-
-    last = pltpu.make_async_copy(total, table_grad, sems.at[4])
-    last.start()
+        count = asked[d, 0, CAP]
+        for first in range(0, CAP, 4):
+
+            @pl.when(count > first)
+            def _():
+                for slot in range(first, first + 4, 2):
+                    at = pl.ds(asked[d, 0, slot], 1)
+                    at2 = pl.ds(asked[d, 0, slot + 1], 1)
+                    total[at, :] += stage[slot : slot + 1, :]
+                    other[at2, :] += stage[slot + 1 : slot + 2, :]
+
+    cut = ROWS // 8
+    for r in range(0, ROWS, cut):
+
+        @pl.loop(r, r + cut, step=128)
+        def _(q):
+            total[pl.ds(q, 128), :] += other[pl.ds(q, 128), :]
+
+        at = pl.ds(r, cut)
+        copies.append(pltpu.make_async_copy(total.at[at], table_grad.at[at], sems.at[7 + r // cut]))
+        copies[-1].start()
     for copy in copies:
         copy.wait()
-    last.wait()
-
-
-def update(asked, returned, summed):
+
+
+def update(asked, returned, summed, loss):
     vmem = pl.BlockSpec(memory_space=pltpu.VMEM)
     hbm = pl.BlockSpec(memory_space=pl.ANY)
     in_shape = jax.ShapeDtypeStruct((WIDTH, HIDDEN), f32)
     out_shape = jax.ShapeDtypeStruct((HIDDEN, WIDTH), f32)
+    table_shape = jax.ShapeDtypeStruct((ROWS, WIDTH), f32)
+    loss_shape = jax.ShapeDtypeStruct((1, PAIRS), f32)
     return pl.pallas_call(
         update_kernel,
-        out_shape=(jax.ShapeDtypeStruct((ROWS, WIDTH), f32), in_shape, out_shape, in_shape, out_shape),
-        in_specs=[pl.BlockSpec(memory_space=pltpu.SMEM), vmem, vmem],
-        out_specs=(hbm,) * 5,
+        out_shape=(table_shape, in_shape, out_shape, in_shape, out_shape, loss_shape),
+        in_specs=[hbm, hbm, hbm, vmem],
+        out_specs=(hbm,) * 5 + (vmem,),
         scratch_shapes=[
+            pltpu.SMEM((SHARDS, 1, SHARDS), jnp.int32),
+            pltpu.VMEM((SHARDS, CAP, WIDTH), bf16),
+            pltpu.VMEM((GRAD_ROWS, WIDTH), bf16),
+            pltpu.VMEM((ROWS, WIDTH), f32),
             pltpu.VMEM((ROWS, WIDTH), f32),
             pltpu.VMEM((2, WIDTH, HIDDEN), f32),
             pltpu.VMEM((2, HIDDEN, WIDTH), f32),
             pltpu.VMEM((CAP, WIDTH), f32),
-            pltpu.SemaphoreType.DMA((5,)),
+            pltpu.SemaphoreType.DMA((15,)),
         ],
-        compiler_params=pltpu.CompilerParams(vmem_limit_bytes=40 << 20),
-    )(asked, returned, summed)
+        compiler_params=pltpu.CompilerParams(vmem_limit_bytes=56 << 20),
+    )(asked, returned, summed, loss)
 
 
 def local(table, feature_owner, feature_offset, query_in, query_out, item_in, item_out):
     loss, asked, returned, summed = train_step(
-        feature_owner, feature_offset, table, query_in, query_out, item_in, item_out
+        feature_owner.T, feature_offset.T, table, query_in, query_out, item_in, item_out
     )
-    table_grad, q_in, q_out, k_in, k_out = update(asked, returned, summed)
+    table_grad, q_in, q_out, k_in, k_out, loss = update(asked, returned, summed, loss)
     return (loss.reshape(PAIRS), table_grad, q_in, q_out, k_in, k_out)
 
 

time: 127 us -> 109 us (0.86)
  the two profiles are of different devices: /device:TPU:25 before, /device:TPU:1 now
where the time goes in v3:
time: 109 us
  Pallas kernels  108 us (99%)
    pallas_call x1, Pallas kernels, train_step(): pl.pallas_call(step_kernel, out_shape=(jax.ShapeDtypeStruct((1, PAIRS), f...  94 us
    pallas_call x1, Pallas kernels, update(): pl.pallas_call(update_kernel, out_shape=(table_shape, in_shape, out_shape...  14.5 us

profile of v3, /device:TPU:1, one launch (start us, length us, event | category | flops | bytes accessed | tf_op | source)
XLA Modules:
  0.0 109.1 jit_solution(6598058271322491549)
XLA Ops:
  0.6 94.0 %shard_map.118 = (f32[1,128]{1,0:T(1,128)}, s32[128,1,128]{2,1,0:T(1,128)}, bf16[128,16,256]{2,1,0:T(8,128)(2,1)}, bf16[4096,256]{1,0:T(8,128)(2,1)}) custom-call(s32[8,128]{1,0:T(8,128)} %bitcast.3, s32[8,128]{1,0:T(8,128)} %bitcast.4, f32[8192,256]{1,0:T(8,128)} %table_ref.1, bf16[256,1024]{1,0:T(8,128)(2,1)} %w_ins_ref.1, bf16[1024,256]{1,0:T(8,128)(2,1)} %w_outs_ref.1, ...), custom_call_target="tpu_custom_call" | custom-call | tf_op jit(solution)/shard_map/pallas_call | solution.py:382
  94.6 14.5 %shard_map.119 = (f32[8192,256]{1,0:T(8,128)}, f32[256,1024]{1,0:T(8,128)}, f32[1024,256]{1,0:T(8,128)}, f32[256,1024]{1,0:T(8,128)}, f32[1024,256]{1,0:T(8,128)}, /*index=5*/f32[1,128]{1,0:T(1,128)}) custom-call(s32[128,1,128]{2,1,0:T(1,128)} %get-tuple-element.16.asked_ref, bf16[128,16,256]{2,1,0:T(8,128)(2,1)} %get-tuple-element.17.returned_ref, ...), custom_call_target="tpu_custom_call" | custom-call | tf_op jit(solution)/shard_map/pallas_call | solution.py:508

commit v4 on v3

--- a/solution.py
+++ b/solution.py
@@ -20,7 +20,13 @@
 BLOCK_K = ITEM_PEERS * PAIRS
 GRAD_ROWS = 4 * HIDDEN
 HALF = GRAD_ROWS // 2
-PARTS = ((0, 768, (0, 1, 2)), (768, 768, (2, 0, 1)), (1536, 512, (1, 2, 0)))
+SHARE = HALF // 2
+PARTS = (
+    ((0, 256, (0, 1, 2)), (256, 256, (1, 2, 0)), (512, 512, (2, 0, 1))),
+    ((0, 512, (0, 1, 2)), (512, 256, (1, 2, 0)), (768, 256, (2, 0, 1))),
+)
+N_PARTS = 6
+ID_RUNS = ((1, 32), (32, 64), (64, 96), (96, 128))
 CUTS = (32, 64, 96)
 f32 = jnp.float32
 bf16 = jnp.bfloat16
@@ -36,7 +42,7 @@
     table_rows, w_in, w_out, requests, asked_scalars, stage, rows, fetched, pick, pick_t,
     pre_act, hidden, unit, norm, queries, items, expo, soft, part_sums,
     q_send, q_recv, k_send, k_recv, slots, inputs, grad_out, grad_pre, core_send, core_recv, half, sum1, recv1, recv2, recv3,
-    load_sems, send_sems, recv_sems, ring_send, ring_recv,
+    load_sems, id_recv, send_sems, recv_sems, ring_send, ring_recv,
 ):
     t = lax.axis_index("table")
     dp = lax.axis_index("dp")
@@ -80,7 +86,7 @@
 
     barrier = pltpu.get_barrier_semaphore()
 
-    @pl.loop(1, SHARDS)
+    @pl.loop(1, SHARDS, unroll=4)
     def _(step):
         pl.semaphore_signal(
             barrier, inc=1, device_id=place(lax.rem(me + step, SHARDS)), device_id_type=MESH
@@ -111,31 +117,38 @@
     pl.semaphore_wait(barrier, SHARDS - 1)
 
     others = pl.ds(0, SHARDS - 1)
-    asked[me] = requests[me]
-
-    @pl.loop(1, SHARDS)
-    def _(step):
-        d = lax.rem(me + step, SHARDS)
-        send(requests.at[d], asked.at[me], send_sems.at[0], recv_sems.at[0], place(d))
-
-    wait(asked.at[others], recv_sems.at[0])
-    spread = pltpu.make_async_copy(asked, asked_scalars, load_sems.at[5])
-    spread.start()
-    loads[0].wait()
-    spread.wait()
-
-    def lookup(d):
+    asked[0] = requests[me]
+    for run, (first, last) in enumerate(ID_RUNS):
+
+        @pl.loop(first, last)
+        def _(step):
+            d = lax.rem(me + step, SHARDS)
+            send(requests.at[d], asked.at[step], send_sems.at[0], id_recv.at[run], place(d))
+
+    def lookup(step):
         for slot in range(CAP):
-            stage[slot : slot + 1, :] = table_rows[pl.ds(asked_scalars[d, 0, slot], 1), :]
+            stage[slot : slot + 1, :] = table_rows[pl.ds(asked_scalars[step, 0, slot], 1), :]
         return stage[...].astype(bf16)
 
-    @pl.loop(1, SHARDS)
-    def _(step):
-        d = lax.rem(me + step, SHARDS)
-        rows[d] = lookup(d)
-        send(rows.at[d], fetched.at[me], send_sems.at[1], recv_sems.at[1], place(d))
-
-    fetched[me] = lookup(me)
+    def send_rows(first, last):
+        @pl.loop(first, last)
+        def _(step):
+            rows[step] = lookup(step)
+            d = lax.rem(me + SHARDS - step, SHARDS)
+            send(rows.at[step], fetched.at[me], send_sems.at[1], recv_sems.at[1], place(d))
+
+    for run, (first, last) in enumerate(ID_RUNS):
+        wait(asked.at[pl.ds(first, last - first)], id_recv.at[run])
+        at = pl.ds(first if run else 0, last - first if run else last)
+        spread = pltpu.make_async_copy(asked.at[at], asked_scalars.at[at], load_sems.at[5])
+        spread.start()
+        if run == 0:
+            loads[0].wait()
+        else:
+            send_rows(*ID_RUNS[run - 1])
+        spread.wait()
+    send_rows(*ID_RUNS[-1])
+    fetched[me] = lookup(0)
 
     cut = 512
     rank_b, named_qb, named_kb = (v.astype(f32).astype(bf16) for v in (rank, named_q, named_k))
@@ -231,16 +244,8 @@
         k_send[j - 1] = part_k(c).astype(bf16)
         send(k_send.at[j - 1], k_recv.at[j - 1], send_sems.at[6], recv_sems.at[6], (t, c * QUERY_PEERS + a))
     grad_k = part_k(z) - query_unit
-    wait(q_recv, recv_sems.at[5])
-    for j in range(QUERY_PEERS - 1):
-        grad_q = grad_q + q_recv[j].astype(f32)
-    grad_q = grad_q * own_inverse - item_unit
-    wait(k_recv, recv_sems.at[6])
-    for j in range(ITEM_PEERS - 1):
-        grad_k = grad_k + k_recv[j].astype(f32)
-
-    grad_x = []
-    for i, grad_unit in enumerate((SCALE * grad_q, SCALE * grad_k)):
+
+    def back(i, grad_unit):
         u = unit[i]
         g = ((grad_unit - u * jnp.sum(grad_unit * u, axis=-1, keepdims=True)) / norm[i]).astype(bf16)
         grad_hidden = mm(g, w_out[i], ((1,), (1,)))
@@ -249,110 +254,150 @@
         gp = (grad_hidden * s * (1.0 + pre * (1.0 - s))).astype(bf16)
         grad_out[i] = g
         grad_pre[i] = gp
-        grad_x.append(mm(gp, w_in[i], ((1,), (1,))).astype(bf16))
-
-    def tower_rows(i, block):
-        at = slice(block % 4 * WIDTH, (block % 4 + 1) * WIDTH)
-        if block < 4:
+
+    def share_rows(i, c, block):
+        at = pl.ds(pl.multiple_of((c * 2 + block % 2) * WIDTH, WIDTH), WIDTH)
+        if block < 2:
             return mm(inputs[i], grad_pre[i, :, at], ((0,), (0,)))
         return mm(hidden[i, :, at], grad_out[i], ((0,), (0,)))
 
-    for p, (base, size, axes) in enumerate(PARTS):
-        for r in range(base, base + size, WIDTH):
-            core_send[r : r + WIDTH] = tower_rows(1 - core, r // WIDTH).astype(bf16)
-        at = pl.ds(base, size)
-        send(core_send.at[at], core_recv.at[at], ring_send.at[p, 0], ring_recv.at[p, 0], chip(coords, 1 - core))
-
-    slots[...] = (
-        mm(pick_t[...], jnp.concatenate(grad_x, axis=0)).astype(bf16).reshape(SHARDS, CAP, WIDTH)
-    )
+    def along(axis, j):
+        moved = list(coords)
+        moved[axis] = lax.rem(coords[axis] + j, 4)
+        return moved[axis], chip(moved, core)
+
+    def rows_at(start, size):
+        return pl.ds(pl.multiple_of(start, 16), size)
+
+    parts = ([], [])
+    at1, at2 = 0, 0
+    for i in range(2):
+        for base, size, axes in PARTS[i]:
+            parts[i].append((len(parts[0]) + len(parts[1]), i * SHARE + base, size, axes, at1, at2))
+            at1, at2 = at1 + size // 4, at2 + size // 16
+
+    def final(i, base):
+        return i * HALF + core * SHARE + base - i * SHARE
+
+    def give_core(i):
+        for p, base, size, axes, at1, at2 in parts[i]:
+            for r in range(base, base + size, WIDTH):
+                block = (r - i * SHARE) // WIDTH
+                core_send[r : r + WIDTH] = share_rows(i, 1 - core, block).astype(bf16)
+            at = pl.ds(base, size)
+            send(core_send.at[at], core_recv.at[at], ring_send.at[p, 0], ring_recv.at[p, 0], chip(coords, 1 - core))
+
+    def step1(i):
+        for p, base, size, axes, at1, at2 in parts[i]:
+            n = size // 4
+            own = [share_rows(i, core, (r - i * SHARE) // WIDTH) for r in range(base, base + size, WIDTH)]
+            wait(core_recv.at[pl.ds(base, size)], ring_recv.at[p, 0])
+            for k, r in enumerate(range(base, base + size, WIDTH)):
+                half[r : r + WIDTH] = (own[k] + core_recv[r : r + WIDTH].astype(f32)).astype(bf16)
+            for j in range(1, 4):
+                c, device = along(axes[0], j)
+                send(half.at[rows_at(base + c * n, n)], recv1.at[j - 1, pl.ds(at1, n)],
+                     ring_send.at[p, 1], ring_recv.at[p, 1], device)
+
+    def step2(i):
+        for p, base, size, axes, at1, at2 in parts[i]:
+            n, m = size // 4, size // 16
+            at = pl.ds(at1, n)
+            wait(recv1.at[:, at], ring_recv.at[p, 1])
+            total1 = half[rows_at(base + coords[axes[0]] * n, n)].astype(f32)
+            for j in range(3):
+                total1 = total1 + recv1[j, at].astype(f32)
+            sum1[at] = total1.astype(bf16)
+            for j in range(1, 4):
+                c, device = along(axes[1], j)
+                send(sum1.at[rows_at(at1 + c * m, m)], recv2.at[j - 1, pl.ds(at2, m)],
+                     ring_send.at[p, 2], ring_recv.at[p, 2], device)
+
+    def step3(i):
+        for p, base, size, axes, at1, at2 in parts[i]:
+            m = size // 16
+            at = pl.ds(at2, m)
+            wait(recv2.at[:, at], ring_recv.at[p, 2])
+            total2 = sum1[rows_at(at1 + coords[axes[1]] * m, m)].astype(f32)
+            for j in range(3):
+                total2 = total2 + recv2[j, at].astype(f32)
+            c3 = coords[axes[2]]
+            recv3[c3, at] = total2.astype(bf16)
+            for j in range(1, 4):
+                _, device = along(axes[2], j)
+                send(recv3.at[c3, at], recv3.at[c3, at], ring_send.at[p, 3], ring_recv.at[p, 3], device)
+
+    def step4(i):
+        for p, base, size, axes, at1, at2 in parts[i]:
+            n, m = size // 4, size // 16
+            at = pl.ds(at2, m)
+            wait(recv3.at[pl.ds(0, 3), at], ring_recv.at[p, 3])
+            total3 = recv3[0, at].astype(f32)
+            for j in range(1, 4):
+                total3 = total3 + recv3[j, at].astype(f32)
+            mine = rows_at(final(i, base) + coords[axes[0]] * n + coords[axes[1]] * m, m)
+            summed[mine] = total3.astype(bf16)
+            for j in range(1, 4):
+                _, device = along(axes[1], j)
+                send(summed.at[mine], summed.at[mine], ring_send.at[p, 4], ring_recv.at[p, 4], device)
+
+    def step5(i):
+        for p, base, size, axes, at1, at2 in parts[i]:
+            n, m = size // 4, size // 16
+            wait(summed.at[pl.ds(0, 3 * m)], ring_recv.at[p, 4])
+            mine = rows_at(final(i, base) + coords[axes[0]] * n, n)
+            for j in range(1, 4):
+                _, device = along(axes[0], j)
+                send(summed.at[mine], summed.at[mine], ring_send.at[p, 4 + j], ring_recv.at[p, 4 + j], device)
+            send(summed.at[mine], summed.at[mine], ring_send.at[p, 8], ring_recv.at[p, 8], chip(coords, 1 - core))
+
+    def step6(i):
+        for j in (1, 3, 2):
+            for p, base, size, axes, at1, at2 in parts[i]:
+                n = size // 4
+                wait(summed.at[pl.ds(0, n)], ring_recv.at[p, 4 + j])
+                there = rows_at(final(i, base) + lax.rem(coords[axes[0]] + 4 - j, 4) * n, n)
+                send(summed.at[there], summed.at[there], ring_send.at[p, 8], ring_recv.at[p, 8], chip(coords, 1 - core))
 
     def send_slots(first, last):
         @pl.loop(first, last)
         def _(step):
             d = lax.rem(me + step, SHARDS)
-            send(slots.at[d], returned.at[me], send_sems.at[7], recv_sems.at[7], place(d))
-
+            send(slots.at[d], returned.at[step], send_sems.at[7], recv_sems.at[7], place(d))
+
+    wait(q_recv, recv_sems.at[5])
+    for j in range(QUERY_PEERS - 1):
+        grad_q = grad_q + q_recv[j].astype(f32)
+    back(0, SCALE * (grad_q * own_inverse - item_unit))
+    give_core(0)
+    step1(0)
+    wait(k_recv, recv_sems.at[6])
+    for j in range(ITEM_PEERS - 1):
+        grad_k = grad_k + k_recv[j].astype(f32)
+    back(1, SCALE * grad_k)
+    give_core(1)
+
+    grad_x = [mm(grad_pre[i], w_in[i], ((1,), (1,))).astype(bf16) for i in range(2)]
+    slots[...] = (
+        mm(pick_t[...], jnp.concatenate(grad_x, axis=0)).astype(bf16).reshape(SHARDS, CAP, WIDTH)
+    )
     send_slots(1, CUTS[0])
-    returned[me] = slots[me]
-
-    def along(axis, j):
-        moved = list(coords)
-        moved[axis] = lax.rem(coords[axis] + j, 4)
-        return moved[axis], chip(moved, core)
-
-    def rows_at(start, size):
-        return pl.ds(pl.multiple_of(start, 16), size)
-
-    at1, at2 = 0, 0
-    spans = []
-    for base, size, _ in PARTS:
-        spans.append((at1, at2))
-        at1, at2 = at1 + size // 4, at2 + size // 16
-    for p, (base, size, axes) in enumerate(PARTS):
-        n = size // 4
-        wait(core_recv.at[pl.ds(base, size)], ring_recv.at[p, 0])
-        for r in range(base, base + size, WIDTH):
-            at = slice(r, r + WIDTH)
-            half[at] = (tower_rows(core, r // WIDTH) + core_recv[at].astype(f32)).astype(bf16)
-        for j in range(1, 4):
-            c, device = along(axes[0], j)
-            send(half.at[rows_at(base + c * n, n)], recv1.at[j - 1, pl.ds(spans[p][0], n)],
-                 ring_send.at[p, 1], ring_recv.at[p, 1], device)
+    returned[0] = slots[me]
+    step1(1)
+    step2(0)
     send_slots(CUTS[0], CUTS[1])
-    for p, (base, size, axes) in enumerate(PARTS):
-        n, m = size // 4, size // 16
-        at = pl.ds(spans[p][0], n)
-        wait(recv1.at[:, at], ring_recv.at[p, 1])
-        total1 = half[rows_at(base + coords[axes[0]] * n, n)].astype(f32)
-        for j in range(3):
-            total1 = total1 + recv1[j, at].astype(f32)
-        sum1[at] = total1.astype(bf16)
-        for j in range(1, 4):
-            c, device = along(axes[1], j)
-            send(sum1.at[rows_at(spans[p][0] + c * m, m)], recv2.at[j - 1, pl.ds(spans[p][1], m)],
-                 ring_send.at[p, 2], ring_recv.at[p, 2], device)
+    step2(1)
+    step3(0)
     send_slots(CUTS[1], CUTS[2])
-    for p, (base, size, axes) in enumerate(PARTS):
-        m = size // 16
-        at = pl.ds(spans[p][1], m)
-        wait(recv2.at[:, at], ring_recv.at[p, 2])
-        total2 = sum1[rows_at(spans[p][0] + coords[axes[1]] * m, m)].astype(f32)
-        for j in range(3):
-            total2 = total2 + recv2[j, at].astype(f32)
-        c3 = coords[axes[2]]
-        recv3[c3, at] = total2.astype(bf16)
-        for j in range(1, 4):
-            _, device = along(axes[2], j)
-            send(recv3.at[c3, at], recv3.at[c3, at], ring_send.at[p, 3], ring_recv.at[p, 3], device)
+    step3(1)
+    step4(0)
     send_slots(CUTS[2], SHARDS)
-    for p, (base, size, axes) in enumerate(PARTS):
-        n, m = size // 4, size // 16
-        at = pl.ds(spans[p][1], m)
-        wait(recv3.at[pl.ds(0, 3), at], ring_recv.at[p, 3])
-        total3 = recv3[0, at].astype(f32)
-        for j in range(1, 4):
-            total3 = total3 + recv3[j, at].astype(f32)
-        mine = rows_at(core * HALF + base + coords[axes[0]] * n + coords[axes[1]] * m, m)
-        summed[mine] = total3.astype(bf16)
-        for j in range(1, 4):
-            _, device = along(axes[1], j)
-            send(summed.at[mine], summed.at[mine], ring_send.at[p, 4], ring_recv.at[p, 4], device)
-    for p, (base, size, axes) in enumerate(PARTS):
-        n, m = size // 4, size // 16
-        wait(summed.at[pl.ds(0, 3 * m)], ring_recv.at[p, 4])
-        mine = rows_at(core * HALF + base + coords[axes[0]] * n, n)
-        for j in range(1, 4):
-            _, device = along(axes[0], j)
-            send(summed.at[mine], summed.at[mine], ring_send.at[p, 4 + j], ring_recv.at[p, 4 + j], device)
-        send(summed.at[mine], summed.at[mine], ring_send.at[p, 8], ring_recv.at[p, 8], chip(coords, 1 - core))
-    for j in (1, 3, 2):
-        for p, (base, size, axes) in enumerate(PARTS):
-            n = size // 4
-            wait(summed.at[pl.ds(0, n)], ring_recv.at[p, 4 + j])
-            there = rows_at(core * HALF + base + lax.rem(coords[axes[0]] + 4 - j, 4) * n, n)
-            send(summed.at[there], summed.at[there], ring_send.at[p, 8], ring_recv.at[p, 8], chip(coords, 1 - core))
-    for p, (base, size, axes) in enumerate(PARTS):
+    step4(1)
+    step5(0)
+    step5(1)
+    step6(0)
+    step6(1)
+    for p, base, size, axes, at1, at2 in parts[0] + parts[1]:
         wait(summed.at[pl.ds(0, size)], ring_recv.at[p, 8])
 
     wait(rows.at[others], recv_sems.at[7])
@@ -367,15 +412,14 @@
         (slots.at[others], 7),
     ):
         wait(ref, send_sems.at[i])
-    for p, (base, size, axes) in enumerate(PARTS):
+    for p, base, size, axes, at1, at2 in parts[0] + parts[1]:
         n, m = size // 4, size // 16
         for i, count in enumerate((size, 3 * n, 3 * m, 3 * m, 3 * m, n, n, n, size)):
             wait(summed.at[pl.ds(0, count)], ring_send.at[p, i])
 
 
 def train_step(owner, offset, table, query_in, query_out, item_in, item_out):
-    rows1 = sum(size // 4 for _, size, _ in PARTS)
-    rows2 = sum(size // 16 for _, size, _ in PARTS)
+    rows1, rows2 = HALF // 4, HALF // 16
     vmem = pl.BlockSpec(memory_space=pltpu.VMEM)
     hbm = pl.BlockSpec(memory_space=pl.ANY)
     V = pltpu.VMEM
@@ -425,10 +469,11 @@
             V((3, rows2, WIDTH), bf16),
             V((4, rows2, WIDTH), bf16),
             pltpu.SemaphoreType.DMA((6,)),
+            pltpu.SemaphoreType.DMA((len(ID_RUNS),)),
             pltpu.SemaphoreType.DMA((8,)),
             pltpu.SemaphoreType.DMA((8,)),
-            pltpu.SemaphoreType.DMA((len(PARTS), 9)),
-            pltpu.SemaphoreType.DMA((len(PARTS), 9)),
+            pltpu.SemaphoreType.DMA((N_PARTS, 9)),
+            pltpu.SemaphoreType.DMA((N_PARTS, 9)),
         ],
         compiler_params=pltpu.CompilerParams(
             collective_id=0, has_side_effects=True, vmem_limit_bytes=56 << 20
@@ -461,8 +506,10 @@
     for i, (out_in, out_out) in enumerate(((q_in, q_out), (k_in, k_out))):
         base = i * HALF
         for c in range(0, HIDDEN, WIDTH):
-            wide_in[i, :, c : c + WIDTH] = summed[base + c : base + c + WIDTH].astype(f32)
-        wide_out[i] = summed[base + HIDDEN : base + HALF].astype(f32)
+            at = base + c // (2 * WIDTH) * SHARE + c % (2 * WIDTH)
+            wide_in[i, :, c : c + WIDTH] = summed[at : at + WIDTH].astype(f32)
+            at += 2 * WIDTH
+            wide_out[i, c : c + WIDTH] = summed[at : at + WIDTH].astype(f32)
         copies.append(pltpu.make_async_copy(wide_in.at[i], out_in, sems.at[3 + 2 * i]))
         copies.append(pltpu.make_async_copy(wide_out.at[i], out_out, sems.at[4 + 2 * i]))
         copies[-2].start()

time: 109 us -> 103 us (0.945)
  Pallas kernels: 108 us -> 102 us
    pallas_call x1, Pallas kernels: 94 us -> 89.9 us  [train_step(): pl.pallas_call(step_kernel, out_shape=(jax.ShapeDtypeStruct((1, PAIRS), f...]
    pallas_call x1, Pallas kernels: 14.5 us -> 11.8 us  [update(): pl.pallas_call(update_kernel, out_shape=(table_shape, in_shape, out_shape...]
where the time goes in v4:
time: 103 us; the launch traced here: 102 us
  Pallas kernels  102 us (99%)
    pallas_call x1, Pallas kernels, train_step(): pl.pallas_call(step_kernel, out_shape=(jax.ShapeDtypeStruct((1, PAIRS), f...  89.9 us
    pallas_call x1, Pallas kernels, update(): pl.pallas_call(update_kernel, out_shape=(table_shape, in_shape, out_shape...  11.8 us

profile of v4, /device:TPU:1, one launch (start us, length us, event | category | flops | bytes accessed | tf_op | source)
XLA Modules:
  0.0 102.3 jit_solution(284793134313616105)
XLA Ops:
  0.6 89.9 %shard_map.118 = (f32[1,128]{1,0:T(1,128)}, s32[128,1,128]{2,1,0:T(1,128)}, bf16[128,16,256]{2,1,0:T(8,128)(2,1)}, bf16[4096,256]{1,0:T(8,128)(2,1)}) custom-call(s32[8,128]{1,0:T(8,128)} %bitcast.3, s32[8,128]{1,0:T(8,128)} %bitcast.4, f32[8192,256]{1,0:T(8,128)} %table_ref.1, bf16[256,1024]{1,0:T(8,128)(2,1)} %w_ins_ref.1, bf16[1024,256]{1,0:T(8,128)(2,1)} %w_outs_ref.1, ...), custom_call_target="tpu_custom_call" | custom-call | tf_op jit(solution)/shard_map/pallas_call | solution.py:426
  90.5 11.8 %shard_map.119 = (f32[8192,256]{1,0:T(8,128)}, f32[256,1024]{1,0:T(8,128)}, f32[1024,256]{1,0:T(8,128)}, f32[256,1024]{1,0:T(8,128)}, f32[1024,256]{1,0:T(8,128)}, /*index=5*/f32[1,128]{1,0:T(1,128)}) custom-call(s32[128,1,128]{2,1,0:T(1,128)} %get-tuple-element.16.asked_ref, bf16[128,16,256]{2,1,0:T(8,128)(2,1)} %get-tuple-element.17.returned_ref, ...), custom_call_target="tpu_custom_call" | custom-call | tf_op jit(solution)/shard_map/pallas_call | solution.py:555

commit v5 on v4

--- a/solution.py
+++ b/solution.py
@@ -1,3 +1,5 @@
+import functools
+
 import jax
 import jax.numpy as jnp
 from jax import lax
@@ -8,6 +10,7 @@
 MESH = pl.DeviceIdType.MESH
 SCALE = 20.0
 SHARDS = 128
+N_TABLE = 4
 GROUP = 32
 CAP = 16
 PAIRS = 128
@@ -26,8 +29,6 @@
     ((0, 512, (0, 1, 2)), (512, 256, (1, 2, 0)), (768, 256, (2, 0, 1))),
 )
 N_PARTS = 6
-ID_RUNS = ((1, 32), (32, 64), (64, 96), (96, 128))
-CUTS = (32, 64, 96)
 f32 = jnp.float32
 bf16 = jnp.bfloat16
 
@@ -38,11 +39,11 @@
 
 def step_kernel(
     owner_ref, offset_ref, table_ref, w_ins_ref, w_outs_ref, w_ini_ref, w_outi_ref,
-    loss_ref, asked, returned, summed,
-    table_rows, w_in, w_out, requests, asked_scalars, stage, rows, fetched, pick, pick_t,
+    loss_ref, asked, returned_out, summed_out,
+    returned, summed, table_rows, w_in, w_out, requests, asked_scalars, stage, rows, fetched, pick, pick_t,
     pre_act, hidden, unit, norm, queries, items, expo, soft, part_sums,
     q_send, q_recv, k_send, k_recv, slots, inputs, grad_out, grad_pre, core_send, core_recv, half, sum1, recv1, recv2, recv3,
-    load_sems, id_recv, send_sems, recv_sems, ring_send, ring_recv,
+    load_sems, id_recv, send_sems, recv_sems, ring_send, ring_recv, store_sems,
 ):
     t = lax.axis_index("table")
     dp = lax.axis_index("dp")
@@ -54,8 +55,19 @@
     y = lax.rem(a, 2) * 2 + lax.div(t, 2)
     coords = (x, y, z)
 
-    def place(device):
-        return (lax.div(device, GROUP), lax.rem(device, GROUP))
+    def each_ahead(u, body, first=0, last=GROUP):
+        tu = lax.rem(t + u, N_TABLE)
+
+        @pl.loop(max(first, 0 if u else 1), last, unroll=4)
+        def _(v):
+            body(u * GROUP + v, tu, lax.rem(dp + v, GROUP))
+
+    def each_behind(u, body):
+        tu = lax.rem(t + N_TABLE - u, N_TABLE)
+
+        @pl.loop(0 if u else 1, GROUP)
+        def _(v):
+            body(u * GROUP + v, tu, lax.rem(dp + GROUP - v, GROUP))
 
     def chip(coords, core):
         cx, cy, cz = coords
@@ -86,11 +98,11 @@
 
     barrier = pltpu.get_barrier_semaphore()
 
-    @pl.loop(1, SHARDS, unroll=4)
-    def _(step):
-        pl.semaphore_signal(
-            barrier, inc=1, device_id=place(lax.rem(me + step, SHARDS)), device_id_type=MESH
-        )
+    def greet(step, tu, dv):
+        pl.semaphore_signal(barrier, inc=1, device_id=(tu, dv), device_id_type=MESH)
+
+    for u in range(N_TABLE):
+        each_ahead(u, greet)
 
     lane = lax.broadcasted_iota(jnp.int32, (PAIRS, SHARDS), 1)
     row = lax.broadcasted_iota(jnp.int32, (PAIRS, SHARDS), 0)
@@ -118,36 +130,34 @@
 
     others = pl.ds(0, SHARDS - 1)
     asked[0] = requests[me]
-    for run, (first, last) in enumerate(ID_RUNS):
-
-        @pl.loop(first, last)
-        def _(step):
-            d = lax.rem(me + step, SHARDS)
-            send(requests.at[d], asked.at[step], send_sems.at[0], id_recv.at[run], place(d))
+
+    def ask(u, step, tu, dv):
+        send(requests.at[tu * GROUP + dv], asked.at[step], send_sems.at[0], id_recv.at[u], (tu, dv))
+
+    for u in range(N_TABLE):
+        each_ahead(u, functools.partial(ask, u))
 
     def lookup(step):
         for slot in range(CAP):
             stage[slot : slot + 1, :] = table_rows[pl.ds(asked_scalars[step, 0, slot], 1), :]
         return stage[...].astype(bf16)
 
-    def send_rows(first, last):
-        @pl.loop(first, last)
-        def _(step):
-            rows[step] = lookup(step)
-            d = lax.rem(me + SHARDS - step, SHARDS)
-            send(rows.at[step], fetched.at[me], send_sems.at[1], recv_sems.at[1], place(d))
-
-    for run, (first, last) in enumerate(ID_RUNS):
-        wait(asked.at[pl.ds(first, last - first)], id_recv.at[run])
-        at = pl.ds(first if run else 0, last - first if run else last)
+    def answer(step, tu, dv):
+        rows[step] = lookup(step)
+        send(rows.at[step], fetched.at[me], send_sems.at[1], recv_sems.at[1], (tu, dv))
+
+    for u in range(N_TABLE):
+        first = u * GROUP if u else 1
+        wait(asked.at[pl.ds(first, (u + 1) * GROUP - first)], id_recv.at[u])
+        at = pl.ds(u * GROUP, GROUP)
         spread = pltpu.make_async_copy(asked.at[at], asked_scalars.at[at], load_sems.at[5])
         spread.start()
-        if run == 0:
+        if u == 0:
             loads[0].wait()
         else:
-            send_rows(*ID_RUNS[run - 1])
+            each_behind(u - 1, answer)
         spread.wait()
-    send_rows(*ID_RUNS[-1])
+    each_behind(N_TABLE - 1, answer)
     fetched[me] = lookup(0)
 
     cut = 512
@@ -359,11 +369,8 @@
                 there = rows_at(final(i, base) + lax.rem(coords[axes[0]] + 4 - j, 4) * n, n)
                 send(summed.at[there], summed.at[there], ring_send.at[p, 8], ring_recv.at[p, 8], chip(coords, 1 - core))
 
-    def send_slots(first, last):
-        @pl.loop(first, last)
-        def _(step):
-            d = lax.rem(me + step, SHARDS)
-            send(slots.at[d], returned.at[step], send_sems.at[7], recv_sems.at[7], place(d))
+    def give_back(step, tu, dv):
+        send(slots.at[tu * GROUP + dv], returned.at[step], send_sems.at[7], recv_sems.at[7], (tu, dv))
 
     wait(q_recv, recv_sems.at[5])
     for j in range(QUERY_PEERS - 1):
@@ -377,30 +384,47 @@
     back(1, SCALE * grad_k)
     give_core(1)
 
+    step1(1)
+
     grad_x = [mm(grad_pre[i], w_in[i], ((1,), (1,))).astype(bf16) for i in range(2)]
     slots[...] = (
         mm(pick_t[...], jnp.concatenate(grad_x, axis=0)).astype(bf16).reshape(SHARDS, CAP, WIDTH)
     )
-    send_slots(1, CUTS[0])
+
+    def give_run(run):
+        each_ahead(run // 2, give_back, run % 2 * (GROUP // 2), (run % 2 + 1) * (GROUP // 2))
+
+    give_run(0)
+    give_run(1)
     returned[0] = slots[me]
-    step1(1)
     step2(0)
-    send_slots(CUTS[0], CUTS[1])
+    give_run(2)
     step2(1)
+    give_run(3)
     step3(0)
-    send_slots(CUTS[1], CUTS[2])
+    give_run(4)
     step3(1)
+    give_run(5)
     step4(0)
-    send_slots(CUTS[2], SHARDS)
+    give_run(6)
     step4(1)
+    give_run(7)
     step5(0)
     step5(1)
     step6(0)
     step6(1)
+    stores = []
     for p, base, size, axes, at1, at2 in parts[0] + parts[1]:
+        i = base // SHARE
         wait(summed.at[pl.ds(0, size)], ring_recv.at[p, 8])
+        for c in range(2):
+            at = pl.ds(i * HALF + c * SHARE + base - i * SHARE, size)
+            stores.append(pltpu.make_async_copy(summed.at[at], summed_out.at[at], store_sems.at[p * 2 + c]))
+            stores[-1].start()
 
     wait(rows.at[others], recv_sems.at[7])
+    stores.append(pltpu.make_async_copy(returned, returned_out, store_sems.at[2 * N_PARTS]))
+    stores[-1].start()
     for ref, i in (
         (requests.at[others], 0),
         (rows.at[others], 1),
@@ -416,6 +440,8 @@
         n, m = size // 4, size // 16
         for i, count in enumerate((size, 3 * n, 3 * m, 3 * m, 3 * m, n, n, n, size)):
             wait(summed.at[pl.ds(0, count)], ring_send.at[p, i])
+    for store in stores:
+        store.wait()
 
 
 def train_step(owner, offset, table, query_in, query_out, item_in, item_out):
@@ -432,8 +458,10 @@
             jax.ShapeDtypeStruct((GRAD_ROWS, WIDTH), bf16),
         ),
         in_specs=[vmem, vmem, hbm, hbm, hbm, hbm, hbm],
-        out_specs=(vmem,) * 4,
+        out_specs=(vmem, vmem, hbm, hbm),
         scratch_shapes=[
+            V((SHARDS, CAP, WIDTH), bf16),
+            V((GRAD_ROWS, WIDTH), bf16),
             V((ROWS, WIDTH), f32),
             V((2, WIDTH, HIDDEN), bf16),
             V((2, HIDDEN, WIDTH), bf16),
@@ -469,11 +497,12 @@
             V((3, rows2, WIDTH), bf16),
             V((4, rows2, WIDTH), bf16),
             pltpu.SemaphoreType.DMA((6,)),
-            pltpu.SemaphoreType.DMA((len(ID_RUNS),)),
+            pltpu.SemaphoreType.DMA((N_TABLE,)),
             pltpu.SemaphoreType.DMA((8,)),
             pltpu.SemaphoreType.DMA((8,)),
             pltpu.SemaphoreType.DMA((N_PARTS, 9)),
             pltpu.SemaphoreType.DMA((N_PARTS, 9)),
+            pltpu.SemaphoreType.DMA((2 * N_PARTS + 1,)),
         ],
         compiler_params=pltpu.CompilerParams(
             collective_id=0, has_side_effects=True, vmem_limit_bytes=56 << 20
@@ -517,19 +546,21 @@
     loads[1].wait()
     loads[2].wait()
 
-    @pl.loop(0, SHARDS)
+    @pl.loop(0, SHARDS, step=2)
     def _(d):
-        stage[...] = returned[d].astype(f32)
-        count = asked[d, 0, CAP]
+        for u in range(2):
+            stage[u] = returned[d + u].astype(f32)
+        count = jnp.maximum(asked[d, 0, CAP], asked[d + 1, 0, CAP])
         for first in range(0, CAP, 4):
 
             @pl.when(count > first)
             def _():
                 for slot in range(first, first + 4, 2):
-                    at = pl.ds(asked[d, 0, slot], 1)
-                    at2 = pl.ds(asked[d, 0, slot + 1], 1)
-                    total[at, :] += stage[slot : slot + 1, :]
-                    other[at2, :] += stage[slot + 1 : slot + 2, :]
+                    for u in range(2):
+                        at = pl.ds(asked[d + u, 0, slot], 1)
+                        at2 = pl.ds(asked[d + u, 0, slot + 1], 1)
+                        total[at, :] += stage[u, slot : slot + 1, :]
+                        other[at2, :] += stage[u, slot + 1 : slot + 2, :]
 
     cut = ROWS // 8
     for r in range(0, ROWS, cut):
@@ -565,7 +596,7 @@
             pltpu.VMEM((ROWS, WIDTH), f32),
             pltpu.VMEM((2, WIDTH, HIDDEN), f32),
             pltpu.VMEM((2, HIDDEN, WIDTH), f32),
-            pltpu.VMEM((CAP, WIDTH), f32),
+            pltpu.VMEM((2, CAP, WIDTH), f32),
             pltpu.SemaphoreType.DMA((15,)),
         ],
         compiler_params=pltpu.CompilerParams(vmem_limit_bytes=56 << 20),

time: 103 us -> 102 us (level)
    pallas_call x1, Pallas kernels: 89.9 us -> 88.6 us  [train_step(): pl.pallas_call(step_kernel, out_shape=(jax.ShapeDtypeStruct((1, PAIRS), f...]
    pallas_call x1, Pallas kernels: 11.8 us -> 13 us  [update(): pl.pallas_call(update_kernel, out_shape=(table_shape, in_shape, out_shape...]
where the time goes in v5:
time: 102 us
  Pallas kernels  102 us (100%)
    pallas_call x1, Pallas kernels, train_step(): pl.pallas_call(step_kernel, out_shape=(jax.ShapeDtypeStruct((1, PAIRS), f...  88.6 us
    pallas_call x1, Pallas kernels, update(): pl.pallas_call(update_kernel, out_shape=(table_shape, in_shape, out_shape...  13 us

profile of v5, /device:TPU:1, one launch (start us, length us, event | category | flops | bytes accessed | tf_op | source)
XLA Modules:
  0.0 102.2 jit_solution(10216282128744376696)
XLA Ops:
  0.6 88.6 %shard_map.118 = (f32[1,128]{1,0:T(1,128)}, s32[128,1,128]{2,1,0:T(1,128)}, bf16[128,16,256]{2,1,0:T(8,128)(2,1)}, bf16[4096,256]{1,0:T(8,128)(2,1)}) custom-call(s32[8,128]{1,0:T(8,128)} %bitcast.3, s32[8,128]{1,0:T(8,128)} %bitcast.4, f32[8192,256]{1,0:T(8,128)} %table_ref.1, bf16[256,1024]{1,0:T(8,128)(2,1)} %w_ins_ref.1, bf16[1024,256]{1,0:T(8,128)(2,1)} %w_outs_ref.1, ...), custom_call_target="tpu_custom_call" | custom-call | tf_op jit(solution)/shard_map/pallas_call | solution.py:452
  89.2 13.0 %shard_map.119 = (f32[8192,256]{1,0:T(8,128)}, f32[256,1024]{1,0:T(8,128)}, f32[1024,256]{1,0:T(8,128)}, f32[256,1024]{1,0:T(8,128)}, f32[1024,256]{1,0:T(8,128)}, /*index=5*/f32[1,128]{1,0:T(1,128)}) custom-call(s32[128,1,128]{2,1,0:T(1,128)} %get-tuple-element.16.asked_ref, bf16[128,16,256]{2,1,0:T(8,128)(2,1)} %get-tuple-element.17.returned_ref, ...), custom_call_target="tpu_custom_call" | custom-call | tf_op jit(solution)/shard_map/pallas_call | solution.py:586

commit v6 on v5

--- a/solution.py
+++ b/solution.py
@@ -39,11 +39,11 @@
 
 def step_kernel(
     owner_ref, offset_ref, table_ref, w_ins_ref, w_outs_ref, w_ini_ref, w_outi_ref,
-    loss_ref, asked, returned_out, summed_out,
-    returned, summed, table_rows, w_in, w_out, requests, asked_scalars, stage, rows, fetched, pick, pick_t,
+    loss_ref, asked_out, returned_out, summed_out,
+    asked, returned, summed, table_rows, w_in, w_out, requests, asked_scalars, stage, rows, fetched, pick, pick_t,
     pre_act, hidden, unit, norm, queries, items, expo, soft, part_sums,
     q_send, q_recv, k_send, k_recv, slots, inputs, grad_out, grad_pre, core_send, core_recv, half, sum1, recv1, recv2, recv3,
-    load_sems, id_recv, send_sems, recv_sems, ring_send, ring_recv, store_sems,
+    load_sems, id_recv, row_recv, send_sems, recv_sems, ring_send, ring_recv, store_sems,
 ):
     t = lax.axis_index("table")
     dp = lax.axis_index("dp")
@@ -64,10 +64,13 @@
 
     def each_behind(u, body):
         tu = lax.rem(t + N_TABLE - u, N_TABLE)
-
-        @pl.loop(0 if u else 1, GROUP)
+        if u == 0:
+            body(0, 1, tu, lax.rem(dp + GROUP - 1, GROUP))
+
+        @pl.loop(0 if u else 2, GROUP, step=2)
         def _(v):
-            body(u * GROUP + v, tu, lax.rem(dp + GROUP - v, GROUP))
+            for k in range(2):
+                body(k, u * GROUP + v + k, tu, lax.rem(dp + GROUP - v - k, GROUP))
 
     def chip(coords, core):
         cx, cy, cz = coords
@@ -137,14 +140,14 @@
     for u in range(N_TABLE):
         each_ahead(u, functools.partial(ask, u))
 
-    def lookup(step):
+    def lookup(k, step):
         for slot in range(CAP):
-            stage[slot : slot + 1, :] = table_rows[pl.ds(asked_scalars[step, 0, slot], 1), :]
-        return stage[...].astype(bf16)
-
-    def answer(step, tu, dv):
-        rows[step] = lookup(step)
-        send(rows.at[step], fetched.at[me], send_sems.at[1], recv_sems.at[1], (tu, dv))
+            stage[k, slot : slot + 1, :] = table_rows[pl.ds(asked_scalars[step, 0, slot], 1), :]
+        return stage[k].astype(bf16)
+
+    def answer(u, k, step, tu, dv):
+        rows[step] = lookup(k, step)
+        send(rows.at[step], fetched.at[me], send_sems.at[1], row_recv.at[u], (tu, dv))
 
     for u in range(N_TABLE):
         first = u * GROUP if u else 1
@@ -155,10 +158,13 @@
         if u == 0:
             loads[0].wait()
         else:
-            each_behind(u - 1, answer)
+            each_behind(u - 1, functools.partial(answer, u - 1))
         spread.wait()
-    each_behind(N_TABLE - 1, answer)
-    fetched[me] = lookup(0)
+    each_behind(N_TABLE - 1, functools.partial(answer, N_TABLE - 1))
+    fetched[me] = lookup(0, 0)
+
+    stores = [pltpu.make_async_copy(asked, asked_out, store_sems.at[2 * N_PARTS + 1])]
+    stores[0].start()
 
     cut = 512
     rank_b, named_qb, named_kb = (v.astype(f32).astype(bf16) for v in (rank, named_q, named_k))
@@ -169,20 +175,17 @@
         hit = mm(rank_b, spread_b) == lax.rem(col, CAP).astype(f32)
         pick[0:PAIRS, c * cut : (c + 1) * cut] = jnp.where(hit, mm(named_qb, spread_b), 0.0).astype(bf16)
         pick[PAIRS:, c * cut : (c + 1) * cut] = jnp.where(hit, mm(named_kb, spread_b), 0.0).astype(bf16)
-        col = lax.broadcasted_iota(jnp.int32, (cut, SHARDS), 0) + c * cut
-        dev = lax.broadcasted_iota(jnp.int32, (cut, SHARDS), 1)
-        spread_b = (lax.div(col, CAP) == dev).astype(bf16)
-        rhs_t = ((1,), (1,))
-        hit = mm(spread_b, rank_b, rhs_t) == lax.rem(col, CAP).astype(f32)
-        pick_t[c * cut : (c + 1) * cut, 0:PAIRS] = jnp.where(hit, mm(spread_b, named_qb, rhs_t), 0.0).astype(bf16)
-        pick_t[c * cut : (c + 1) * cut, PAIRS:] = jnp.where(hit, mm(spread_b, named_kb, rhs_t), 0.0).astype(bf16)
 
     for load in loads[1:]:
         load.wait()
-    wait(rows.at[others], recv_sems.at[1])
-    inputs[...] = (
-        mm(pick[...], fetched[...].reshape(SHARDS * CAP, WIDTH)).astype(bf16).reshape(2, PAIRS, WIDTH)
-    )
+    sums = jnp.zeros((2 * PAIRS, WIDTH), f32)
+    for u in range(N_TABLE):
+        count = GROUP if u else GROUP - 1
+        wait(rows.at[pl.ds(0, count)], row_recv.at[u])
+        tu = lax.rem(t + u, N_TABLE)
+        from_group = fetched[pl.ds(tu * GROUP, GROUP)].reshape(GROUP * CAP, WIDTH)
+        sums = sums + mm(pick[:, pl.ds(pl.multiple_of(tu * GROUP * CAP, GROUP * CAP), GROUP * CAP)], from_group)
+    inputs[...] = sums.astype(bf16).reshape(2, PAIRS, WIDTH)
 
     for i in range(2):
         pre = mm(inputs[i], w_in[i])
@@ -203,6 +206,15 @@
             for j in range(1, ITEM_PEERS):
                 peer = (t, lax.rem(z + j, ITEM_PEERS) * QUERY_PEERS + a)
                 send(items.at[z], items.at[z], send_sems.at[3], recv_sems.at[3], peer)
+    for c in range(SHARDS * CAP // cut):
+        col = lax.broadcasted_iota(jnp.int32, (cut, SHARDS), 0) + c * cut
+        dev = lax.broadcasted_iota(jnp.int32, (cut, SHARDS), 1)
+        spread_b = (lax.div(col, CAP) == dev).astype(bf16)
+        rhs_t = ((1,), (1,))
+        hit = mm(spread_b, rank_b, rhs_t) == lax.rem(col, CAP).astype(f32)
+        pick_t[c * cut : (c + 1) * cut, 0:PAIRS] = jnp.where(hit, mm(spread_b, named_qb, rhs_t), 0.0).astype(bf16)
+        pick_t[c * cut : (c + 1) * cut, PAIRS:] = jnp.where(hit, mm(spread_b, named_kb, rhs_t), 0.0).astype(bf16)
+
     query_unit = queries[a].astype(f32)
     item_unit = items[z].astype(f32)
     wait(items.at[pl.ds(0, ITEM_PEERS - 1)], recv_sems.at[3])
@@ -391,6 +403,13 @@
         mm(pick_t[...], jnp.concatenate(grad_x, axis=0)).astype(bf16).reshape(SHARDS, CAP, WIDTH)
     )
 
+    def wait_sent(first, last):
+        for p, base, size, axes, at1, at2 in parts[0] + parts[1]:
+            n, m = size // 4, size // 16
+            counts = (size, 3 * n, 3 * m, 3 * m, 3 * m, n, n, n, size)
+            for i in range(first, last):
+                wait(summed.at[pl.ds(0, counts[i])], ring_send.at[p, i])
+
     def give_run(run):
         each_ahead(run // 2, give_back, run % 2 * (GROUP // 2), (run % 2 + 1) * (GROUP // 2))
 
@@ -399,6 +418,16 @@
     returned[0] = slots[me]
     step2(0)
     give_run(2)
+    for ref, i in (
+        (requests.at[others], 0),
+        (rows.at[others], 1),
+        (queries.at[pl.ds(0, QUERY_PEERS - 1)], 2),
+        (items.at[pl.ds(0, ITEM_PEERS - 1)], 3),
+        (part_sums.at[pl.ds(0, QUERY_PEERS - 1)], 4),
+        (q_send, 5),
+        (k_send, 6),
+    ):
+        wait(ref, send_sems.at[i])
     step2(1)
     give_run(3)
     step3(0)
@@ -411,9 +440,9 @@
     give_run(7)
     step5(0)
     step5(1)
+    wait_sent(0, 4)
     step6(0)
     step6(1)
-    stores = []
     for p, base, size, axes, at1, at2 in parts[0] + parts[1]:
         i = base // SHARE
         wait(summed.at[pl.ds(0, size)], ring_recv.at[p, 8])
@@ -425,21 +454,8 @@
     wait(rows.at[others], recv_sems.at[7])
     stores.append(pltpu.make_async_copy(returned, returned_out, store_sems.at[2 * N_PARTS]))
     stores[-1].start()
-    for ref, i in (
-        (requests.at[others], 0),
-        (rows.at[others], 1),
-        (queries.at[pl.ds(0, QUERY_PEERS - 1)], 2),
-        (items.at[pl.ds(0, ITEM_PEERS - 1)], 3),
-        (part_sums.at[pl.ds(0, QUERY_PEERS - 1)], 4),
-        (q_send, 5),
-        (k_send, 6),
-        (slots.at[others], 7),
-    ):
-        wait(ref, send_sems.at[i])
-    for p, base, size, axes, at1, at2 in parts[0] + parts[1]:
-        n, m = size // 4, size // 16
-        for i, count in enumerate((size, 3 * n, 3 * m, 3 * m, 3 * m, n, n, n, size)):
-            wait(summed.at[pl.ds(0, count)], ring_send.at[p, i])
+    wait(slots.at[others], send_sems.at[7])
+    wait_sent(4, 9)
     for store in stores:
         store.wait()
 
@@ -458,8 +474,9 @@
             jax.ShapeDtypeStruct((GRAD_ROWS, WIDTH), bf16),
         ),
         in_specs=[vmem, vmem, hbm, hbm, hbm, hbm, hbm],
-        out_specs=(vmem, vmem, hbm, hbm),
+        out_specs=(vmem, hbm, hbm, hbm),
         scratch_shapes=[
+            V((SHARDS, 1, SHARDS), jnp.int32),
             V((SHARDS, CAP, WIDTH), bf16),
             V((GRAD_ROWS, WIDTH), bf16),
             V((ROWS, WIDTH), f32),
@@ -467,7 +484,7 @@
             V((2, HIDDEN, WIDTH), bf16),
             V((SHARDS, 1, SHARDS), jnp.int32),
             pltpu.SMEM((SHARDS, 1, SHARDS), jnp.int32),
-            V((CAP, WIDTH), f32),
+            V((2, CAP, WIDTH), f32),
             V((SHARDS, CAP, WIDTH), bf16),
             V((SHARDS, CAP, WIDTH), bf16),
             V((2 * PAIRS, SHARDS * CAP), bf16),
@@ -498,11 +515,12 @@
             V((4, rows2, WIDTH), bf16),
             pltpu.SemaphoreType.DMA((6,)),
             pltpu.SemaphoreType.DMA((N_TABLE,)),
+            pltpu.SemaphoreType.DMA((N_TABLE,)),
             pltpu.SemaphoreType.DMA((8,)),
             pltpu.SemaphoreType.DMA((8,)),
             pltpu.SemaphoreType.DMA((N_PARTS, 9)),
             pltpu.SemaphoreType.DMA((N_PARTS, 9)),
-            pltpu.SemaphoreType.DMA((2 * N_PARTS + 1,)),
+            pltpu.SemaphoreType.DMA((2 * N_PARTS + 2,)),
         ],
         compiler_params=pltpu.CompilerParams(
             collective_id=0, has_side_effects=True, vmem_limit_bytes=56 << 20

time: 102 us -> 102 us (level)
  no operation moved by 1% of the time
where the time goes in v6:
time: 102 us
  Pallas kernels  101 us (99%)
    pallas_call x1, Pallas kernels, train_step(): pl.pallas_call(step_kernel, out_shape=(jax.ShapeDtypeStruct((1, PAIRS), f...  88 us
    pallas_call x1, Pallas kernels, update(): pl.pallas_call(update_kernel, out_shape=(table_shape, in_shape, out_shape...  13.1 us

profile of v6, /device:TPU:1, one launch (start us, length us, event | category | flops | bytes accessed | tf_op | source)
XLA Modules:
  0.0 101.7 jit_solution(13668744740952342523)
XLA Ops:
  0.6 88.0 %shard_map.118 = (f32[1,128]{1,0:T(1,128)}, s32[128,1,128]{2,1,0:T(1,128)}, bf16[128,16,256]{2,1,0:T(8,128)(2,1)}, bf16[4096,256]{1,0:T(8,128)(2,1)}) custom-call(s32[8,128]{1,0:T(8,128)} %bitcast.3, s32[8,128]{1,0:T(8,128)} %bitcast.4, f32[8192,256]{1,0:T(8,128)} %table_ref.1, bf16[256,1024]{1,0:T(8,128)(2,1)} %w_ins_ref.1, bf16[1024,256]{1,0:T(8,128)(2,1)} %w_outs_ref.1, ...), custom_call_target="tpu_custom_call" | custom-call | tf_op jit(solution)/shard_map/pallas_call | solution.py:468
  88.7 13.1 %shard_map.119 = (f32[8192,256]{1,0:T(8,128)}, f32[256,1024]{1,0:T(8,128)}, f32[1024,256]{1,0:T(8,128)}, f32[256,1024]{1,0:T(8,128)}, f32[1024,256]{1,0:T(8,128)}, /*index=5*/f32[1,128]{1,0:T(1,128)}) custom-call(s32[128,1,128]{2,1,0:T(1,128)} %get-tuple-element.16.asked_ref, bf16[128,16,256]{2,1,0:T(8,128)(2,1)} %get-tuple-element.17.returned_ref, ...), custom_call_target="tpu_custom_call" | custom-call | tf_op jit(solution)/shard_map/pallas_call | solution.py:604

commit v7 on v6

--- a/solution.py
+++ b/solution.py
@@ -569,11 +569,11 @@
         for u in range(2):
             stage[u] = returned[d + u].astype(f32)
         count = jnp.maximum(asked[d, 0, CAP], asked[d + 1, 0, CAP])
-        for first in range(0, CAP, 4):
+        for first in range(0, CAP, 8):
 
             @pl.when(count > first)
             def _():
-                for slot in range(first, first + 4, 2):
+                for slot in range(first, first + 8, 2):
                     for u in range(2):
                         at = pl.ds(asked[d + u, 0, slot], 1)
                         at2 = pl.ds(asked[d + u, 0, slot + 1], 1)

time: 102 us -> 99.4 us (0.975)
  Pallas kernels: 101 us -> 98.6 us
    pallas_call x1, Pallas kernels: 13.1 us -> 10.6 us  [update(): pl.pallas_call(update_kernel, out_shape=(table_shape, in_shape, out_shape...]
where the time goes in v7:
time: 99.4 us; the launch traced here: 99.3 us
  Pallas kernels  98.6 us (99%)
    pallas_call x1, Pallas kernels, train_step(): pl.pallas_call(step_kernel, out_shape=(jax.ShapeDtypeStruct((1, PAIRS), f...  88 us
    pallas_call x1, Pallas kernels, update(): pl.pallas_call(update_kernel, out_shape=(table_shape, in_shape, out_shape...  10.6 us

profile of v7, /device:TPU:1, one launch (start us, length us, event | category | flops | bytes accessed | tf_op | source)
XLA Modules:
  0.0 99.3 jit_solution(5454662732836437525)
XLA Ops:
  0.6 88.0 %shard_map.118 = (f32[1,128]{1,0:T(1,128)}, s32[128,1,128]{2,1,0:T(1,128)}, bf16[128,16,256]{2,1,0:T(8,128)(2,1)}, bf16[4096,256]{1,0:T(8,128)(2,1)}) custom-call(s32[8,128]{1,0:T(8,128)} %bitcast.3, s32[8,128]{1,0:T(8,128)} %bitcast.4, f32[8192,256]{1,0:T(8,128)} %table_ref.1, bf16[256,1024]{1,0:T(8,128)(2,1)} %w_ins_ref.1, bf16[1024,256]{1,0:T(8,128)(2,1)} %w_outs_ref.1, ...), custom_call_target="tpu_custom_call" | custom-call | tf_op jit(solution)/shard_map/pallas_call | solution.py:468
  88.7 10.6 %shard_map.119 = (f32[8192,256]{1,0:T(8,128)}, f32[256,1024]{1,0:T(8,128)}, f32[1024,256]{1,0:T(8,128)}, f32[256,1024]{1,0:T(8,128)}, f32[1024,256]{1,0:T(8,128)}, /*index=5*/f32[1,128]{1,0:T(1,128)}) custom-call(s32[128,1,128]{2,1,0:T(1,128)} %get-tuple-element.16.asked_ref, bf16[128,16,256]{2,1,0:T(8,128)(2,1)} %get-tuple-element.17.returned_ref, ...), custom_call_target="tpu_custom_call" | custom-call | tf_op jit(solution)/shard_map/pallas_call | solution.py:604
